TPU v7x, 32 devices: a whole 2x2x4 slice. The times are simulated.
32 devices in a mesh: py: 4 (over x, core), px: 8 (over z, y).
Axes of the slice: x: 2, y: 2, z: 4, core: 2. Of those that a mesh axis runs over, the one named last changes fastest.
Arguments:
- forcing: float32 [1024, 8, 1024], P('px', 'py')
- inv_density: float32 [1024, 8, 1024], P('px', 'py'), may hold values from 0.5 to 4
- stretch_x: float32 [1024], P('px'), may hold values from 0.5 to 2
- stretch_y: float32 [8], P('py'), may hold values from 0.5 to 2
- stretch_z: float32 [1024], replicated, may hold values from 0.5 to 2
- lines_z0: float32 [4, 256, 256], replicated
- lines_x0: float32 [4, 256, 256], replicated
- lines_z1: float32 [2, 256, 256], replicated
- lines_x1: float32 [2, 256, 256], replicated
- coarse_inverse: float32 [32, 32], P(('py', 'px')), as said below
Outputs:
- pressure_adjoint: float32 [1024, 8, 1024], P('px', 'py')
Inputs may be any that keep to these rules, and one draw needn't show every extreme that they name: coarse_inverse is symmetric.
All inputs are finite; a program needn't handle non-finite values.
Results may differ from a plain program's by a relative error of at most 0.0001.
Values sent between devices are 32-bit elements; how exact they have to be, the bound alone decides.
A program may use at most 128 MiB of HBM per device.

v0:
```python
import jax
import jax.numpy as jnp
from jax import lax
from jax.sharding import PartitionSpec as P

shift_term = 0.1
highest = lax.Precision.HIGHEST


def with_halo(array, sides, width):
    for axis, dim in sides:
        peers, length = (lax.axis_size(axis), array.shape[dim])
        up = [(i, (i + 1) % peers) for i in range(peers - 1)]
        down = [(j, i) for i, j in up]
        last = lax.slice_in_dim(array, length - width, length, axis=dim)
        initial = lax.slice_in_dim(array, 0, width, axis=dim)
        before = lax.ppermute(last, axis, up)
        after = lax.ppermute(initial, axis, down)
        array = jnp.concatenate([before, array, after], axis=dim)
    return array


def pad_axis(field, axis):
    widths = [(0, 0), (0, 0), (0, 0)]
    widths[axis] = (1, 1)
    return jnp.pad(field, widths)


def beside_sum(padded, axis):
    length = padded.shape[axis] - 2
    return lax.slice_in_dim(padded, 2, length + 2, axis=axis) + lax.slice_in_dim(
        padded, 0, length, axis=axis
    )


def with_rim(field):
    return with_halo(field, (("py", 1), ("px", 0)), 1)


def operate(field, level):
    density, coef_x, coef_y, coef_z = (level[0], level[1], level[2], level[3])
    padded = with_rim(field)
    twice = 2.0 * field
    near_x = beside_sum(padded[:, 1:-1], 0)
    near_y = beside_sum(padded[1:-1], 1)
    near_z = beside_sum(pad_axis(field, 2), 2)
    stencil = (
        coef_x[:, None, None] * (twice - near_x)
        + coef_y[None, :, None] * (twice - near_y)
        + coef_z[None, None, :] * (twice - near_z)
    )
    return shift_term * field + density * stencil


def diagonal(density, coef_x, coef_y, coef_z):
    return shift_term + 2.0 * density * (
        coef_x[:, None, None] + coef_y[None, :, None] + coef_z[None, None, :]
    )


def lines_along_z(field, blocks):
    first, second, third = field.shape
    count = blocks.shape[0]
    grouped = field.reshape(first * second, count, third // count)
    return jnp.einsum("nkb,kcb->nkc", grouped, blocks, precision=highest).reshape(
        first, second, third
    )


def lines_along_x(field, blocks):
    piece = lax.all_to_all(field, "px", split_axis=2, concat_axis=0, tiled=True)
    rows, items, depth = piece.shape
    count = blocks.shape[0]
    grouped = piece.reshape(count, rows // count, items * depth)
    solved = jnp.einsum("kcb,kbn->kcn", blocks, grouped, precision=highest).reshape(
        rows, items, depth
    )
    return lax.all_to_all(solved, "px", split_axis=0, concat_axis=2, tiled=True)


def sweep(iterate, rhs, level, from_zero):
    if from_zero:
        residual = rhs
    else:
        residual = rhs - operate(iterate, level)
    iterate = iterate + lines_along_z(residual / level[4], level[5])
    residual = rhs - operate(iterate, level)
    scaled = residual / level[4]
    return iterate + lines_along_x(scaled, level[6])


def restrict_padded(padded, axis):
    length = padded.shape[axis] - 2

    def take(start):
        return lax.slice_in_dim(padded, start, start + length - 1, stride=2, axis=axis)

    return (take(0) + 3.0 * take(1) + 3.0 * take(2) + take(3)) * 0.125


def prolong_padded(padded, axis):
    length = padded.shape[axis] - 2
    lower = lax.slice_in_dim(padded, 0, length, axis=axis)
    middle = lax.slice_in_dim(padded, 1, length + 1, axis=axis)
    upper = lax.slice_in_dim(padded, 2, length + 2, axis=axis)
    even = (3.0 * middle + lower) * 0.25
    odd = (3.0 * middle + upper) * 0.25
    stacked = jnp.stack([even, odd], axis=axis + 1)
    shape = list(even.shape)
    shape[axis] = 2 * length
    return stacked.reshape(shape)


def halve(vector):
    return vector.reshape(-1, 2).sum(axis=1) * 0.125


def coarsen(density, coef_x, coef_y, coef_z):
    first, second, third = density.shape
    dense_one = density.reshape(first // 2, 2, second // 2, 2, third // 2, 2).mean(axis=(1, 3, 5))
    return (dense_one, halve(coef_x), halve(coef_y), halve(coef_z))


def per_device(
    forcing,
    inv_density,
    stretch_x,
    stretch_y,
    stretch_z,
    lines_z0,
    lines_x0,
    lines_z1,
    lines_x1,
    coarse_inverse,
):
    fine = (
        inv_density,
        stretch_x,
        stretch_y,
        stretch_z,
        diagonal(inv_density, stretch_x, stretch_y, stretch_z),
        lines_z0,
        lines_x0,
    )
    dense_one, coef_x1, coef_y1, coef_z1 = coarsen(inv_density, stretch_x, stretch_y, stretch_z)
    middle = (
        dense_one,
        coef_x1,
        coef_y1,
        coef_z1,
        diagonal(dense_one, coef_x1, coef_y1, coef_z1),
        lines_z1,
        lines_x1,
    )
    iterate = jnp.zeros_like(forcing)
    iterate = sweep(iterate, forcing, fine, 0 == 0)
    residual = forcing - operate(iterate, fine)
    padded = with_rim(residual)
    right_one = restrict_padded(restrict_padded(padded, 0), 1)
    right_one = restrict_padded(pad_axis(right_one, 2), 2)
    level_one = sweep(jnp.zeros_like(right_one), right_one, middle, True)
    residual_one = right_one - operate(level_one, middle)
    local_mean = jnp.mean(residual_one)
    correction = lax.psum_scatter(
        coarse_inverse[0] * local_mean, ("py", "px"), scatter_dimension=0, tiled=True
    )[0]
    level_one = level_one + correction
    level_one = sweep(level_one, right_one, middle, False)
    padded = with_rim(level_one)
    raised = prolong_padded(prolong_padded(padded, 0), 1)
    raised = prolong_padded(pad_axis(raised, 2), 2)
    iterate = iterate + raised
    iterate = sweep(iterate, forcing, fine, False)
    return iterate


def solution(mesh):
    placed = (
        P("px", "py", None),
        P("px", "py", None),
        P("px"),
        P("py"),
        P(),
        P(),
        P(),
        P(),
        P(),
        P(("py", "px"), None),
    )
    return jax.shard_map(
        per_device, mesh=mesh, in_specs=placed, out_specs=P("px", "py", None), check_vma=False
    )
```

profile of v0, /device:TPU:0, one launch (start us, length us, event | category | flops | bytes accessed | tf_op | source)
XLA Modules:
  0.0 647.4 jit_solution(4705195331664889119)
XLA Ops:
  32.6 30.7 %all_to_all.132 = f32[128,2,1024]{0,1,2:T(2,128)} all-to-all(f32[128,2,1024]{0,1,2:T(2,128)S(1)} %copy.238), channel_id=1, replica_groups=mesh['py'=4,'px'=8] {'px'}, dimensions={2} | all-to-all | bytes 2097152 | tf_op jit(solution)/shard_map/all_to_all | solution.py:71
  76.7 31.5 %all_to_all.133 = f32[1024,2,128]{2,1,0:T(2,128)S(1)} all-to-all(f32[1024,2,128]{2,1,0:T(2,128)} %reshape.386), channel_id=1, replica_groups=mesh['py'=4,'px'=8] {'px'}, dimensions={0} | all-to-all | bytes 2097152 | tf_op jit(solution)/shard_map/all_to_all | solution.py:78
  129.2 8.6 %collective-permute-start.8 = (f32[128,1,1024]{2,0,1:T(8,128)}, f32[128,1,1024]{2,0,1:T(8,128)}, u32[]{:S(2)}, u32[]{:S(2)}) collective-permute-start(f32[128,1,1024]{2,0,1:T(8,128)} %get-tuple-element.21), channel_id=1, source_target_pairs={{0,8},{8,16},{16,24},{1,9},{9,17},{17,25},{2,10},{10,18},{18,26},{... | collective-permute-start | bytes 1572872 | tf_op jit(solution)/shard_map/ppermute | solution.py:17
  151.7 35.6 %reduce_sum.53 = f32[64,2,512,2]{3,2,1,0:T(8,128)} reshape(f32[128,1024]{1,0:T(8,128)} %reduce_sum.52) | data formatting | bytes 1048576 | tf_op jit(solution)/shard_map/reduce_sum | solution.py:120
  187.3 13.2 %reduce_sum.54 = f32[64,512]{1,0:T(8,128)S(1)} reduce(f32[64,2,512,2]{3,2,1,0:T(8,128)} %reduce_sum.53, f32[]{:T(128)} %constant.9.clone.1), dimensions={1,3}, to_apply=%region_1.0 | reduce | flops 98304 | bytes 655364 | tf_op jit(solution)/shard_map/reduce_sum | solution.py:120
  200.6 5.4 slice.348
  206.0 5.4 slice.347
  214.8 5.5 slice.349
  220.3 5.4 slice.346
  229.2 5.4 slice.357
  234.6 6.0 slice.356
  240.6 5.9 slice.354
  246.5 6.0 slice.355
  258.7 6.8 %collective-permute-start.12 = (f32[64,1,512]{2,0,1:T(8,128)S(1)}, f32[64,1,512]{2,0,1:T(8,128)S(1)}, u32[]{:S(2)}, u32[]{:S(2)}) collective-permute-start(f32[64,1,512]{2,0,1:T(8,128)S(1)} %reshape.390), channel_id=1, source_target_pairs={{0,8},{8,16},{16,24},{1,9},{9,17},{17,25},{2,10},{10,18},{18,26},{... | collective-permute-start | bytes 393224 | tf_op jit(solution)/shard_map/ppermute | solution.py:17
  289.7 11.3 %all_to_all.134 = f32[8,1,4096]{2,1,0:T(1,128)} all-to-all(f32[8,1,4096]{2,1,0:T(1,128)} %reshape.404), channel_id=1, replica_groups=mesh['py'=4,'px'=8] {'px'}, dimensions={0} | all-to-all | bytes 262144 | tf_op jit(solution)/shard_map/all_to_all | solution.py:71
  318.1 11.4 %all_to_all.135 = f32[8,1,4096]{2,1,0:T(1,128)} all-to-all(f32[8,1,4096]{2,1,0:T(1,128)S(1)} %reshape.406), channel_id=1, replica_groups=mesh['py'=4,'px'=8] {'px'}, dimensions={0} | all-to-all | bytes 262144 | tf_op jit(solution)/shard_map/all_to_all | solution.py:78
  356.3 44.0 %all-reduce.10 = f32[32]{0:T(128)} all-reduce(f32[32]{0:T(128)} %multiply_bitcast_fusion), channel_id=2, replica_groups=mesh['py'=4,'px'=8] {'py','px'}, use_global_device_ids=true, to_apply=%region_6.7.clone | all-reduce | flops 32 | bytes 256
  446.5 10.7 %all_to_all.136 = f32[8,1,4096]{2,1,0:T(1,128)S(1)} all-to-all(f32[8,1,4096]{2,1,0:T(1,128)S(1)} %reshape.408), channel_id=1, replica_groups=mesh['py'=4,'px'=8] {'px'}, dimensions={0} | all-to-all | bytes 262144 | tf_op jit(solution)/shard_map/all_to_all | solution.py:71
  467.0 10.2 %all_to_all.137 = f32[8,1,4096]{2,1,0:T(1,128)S(1)} all-to-all(f32[8,1,4096]{2,1,0:T(1,128)S(1)} %reshape.410), channel_id=1, replica_groups=mesh['py'=4,'px'=8] {'px'}, dimensions={0} | all-to-all | bytes 262144 | tf_op jit(solution)/shard_map/all_to_all | solution.py:78
  509.8 7.4 %collective-permute-start.32 = (f32[128,1,1024]{2,0,1:T(8,128)S(1)}, f32[128,1,1024]{2,0,1:T(8,128)S(1)}, u32[]{:S(2)}, u32[]{:S(2)}) collective-permute-start(f32[128,1,1024]{2,0,1:T(8,128)S(1)} %get-tuple-element.20), channel_id=1, source_target_pairs={{0,8},{8,16},{16,24},{1,9},{9,17},{17,25},{2,10},{10,18},{18,26},{... | collective-permute-start | bytes 1572872 | tf_op jit(solution)/shard_map/ppermute | solution.py:17
  518.7 5.7 collective-permute-done.33
  546.1 7.8 %collective-permute-start.36 = (f32[128,1,1024]{2,0,1:T(8,128)S(1)}, f32[128,1,1024]{2,0,1:T(8,128)S(1)}, u32[]{:S(2)}, u32[]{:S(2)}) collective-permute-start(f32[128,1,1024]{2,0,1:T(8,128)S(1)} %get-tuple-element.18), channel_id=1, source_target_pairs={{0,8},{8,16},{16,24},{1,9},{9,17},{17,25},{2,10},{10,18},{18,26},{... | collective-permute-start | bytes 1572872 | tf_op jit(solution)/shard_map/ppermute | solution.py:17
  572.0 28.2 %all_to_all.138 = f32[128,2,1024]{0,1,2:T(2,128)} all-to-all(f32[128,2,1024]{0,1,2:T(2,128)S(1)} %copy.279), channel_id=1, replica_groups=mesh['py'=4,'px'=8] {'px'}, dimensions={2} | all-to-all | bytes 2097152 | tf_op jit(solution)/shard_map/all_to_all | solution.py:71
  613.6 31.4 %all_to_all.139 = f32[1024,2,128]{2,1,0:T(2,128)S(1)} all-to-all(f32[1024,2,128]{2,1,0:T(2,128)} %reshape.403), channel_id=1, replica_groups=mesh['py'=4,'px'=8] {'px'}, dimensions={0} | all-to-all | bytes 2097152 | tf_op jit(solution)/shard_map/all_to_all | solution.py:78
  (254 shorter events, 305.2 us)
Async XLA Ops:
  13.4 6.0 collective-permute-start.1
  22.9 5.6 collective-permute-start.2
  118.2 5.6 collective-permute-start.6
  127.9 11.8 %collective-permute-start.9 = (f32[128,1,1024]{2,0,1:T(8,128)}, f32[128,1,1024]{2,0,1:T(8,128)}, u32[]{:S(2)}, u32[]{:S(2)}) collective-permute-start(f32[128,1,1024]{2,0,1:T(8,128)} %get-tuple-element.22), channel_id=1, source_target_pairs={{8,0},{16,8},{24,16},{9,1},{17,9},{25,17},{10,2},{18,10},{26,18},{... | collective-permute-start | bytes 1572872 | tf_op jit(solution)/shard_map/ppermute | solution.py:18
  129.2 10.5 %collective-permute-start.8 = (f32[128,1,1024]{2,0,1:T(8,128)}, f32[128,1,1024]{2,0,1:T(8,128)}, u32[]{:S(2)}, u32[]{:S(2)}) collective-permute-start(f32[128,1,1024]{2,0,1:T(8,128)} %get-tuple-element.21), channel_id=1, source_target_pairs={{0,8},{8,16},{16,24},{1,9},{9,17},{17,25},{2,10},{10,18},{18,26},{... | collective-permute-start | bytes 1572872 | tf_op jit(solution)/shard_map/ppermute | solution.py:17
  142.7 68.6 %collective-permute-start.11 = (f32[1,4,1024]{2,0,1:T(1,128)S(1)}, f32[1,4,1024]{2,0,1:T(1,128)S(1)}, u32[]{:S(2)}, u32[]{:S(2)}) collective-permute-start(f32[1,4,1024]{2,0,1:T(1,128)S(1)} %get-tuple-element.12), channel_id=1, source_target_pairs={{1,0},{2,1},{3,2},{4,3},{5,4},{6,5},{7,6},{9,8},{10,9},{11,10},{12... | collective-permute-start | bytes 49160 | tf_op jit(solution)/shard_map/ppermute | solution.py:18
  144.0 67.3 %collective-permute-start.10 = (f32[1,4,1024]{2,0,1:T(1,128)S(1)}, f32[1,4,1024]{2,0,1:T(1,128)S(1)}, u32[]{:S(2)}, u32[]{:S(2)}) collective-permute-start(f32[1,4,1024]{2,0,1:T(1,128)S(1)} %get-tuple-element.11), channel_id=1, source_target_pairs={{0,1},{1,2},{2,3},{3,4},{4,5},{5,6},{6,7},{8,9},{9,10},{10,11},{11... | collective-permute-start | bytes 49160 | tf_op jit(solution)/shard_map/ppermute | solution.py:17
  258.7 8.1 %collective-permute-start.12 = (f32[64,1,512]{2,0,1:T(8,128)S(1)}, f32[64,1,512]{2,0,1:T(8,128)S(1)}, u32[]{:S(2)}, u32[]{:S(2)}) collective-permute-start(f32[64,1,512]{2,0,1:T(8,128)S(1)} %reshape.390), channel_id=1, source_target_pairs={{0,8},{8,16},{16,24},{1,9},{9,17},{17,25},{2,10},{10,18},{18,26},{... | collective-permute-start | bytes 393224 | tf_op jit(solution)/shard_map/ppermute | solution.py:17
  265.5 5.8 collective-permute-start.13
  271.3 6.0 collective-permute-start.15
  275.8 5.5 collective-permute-start.14
  346.9 5.8 collective-permute-start.18
  407.6 5.7 collective-permute-start.23
  411.9 5.5 collective-permute-start.22
  431.6 5.0 collective-permute-start.27
  435.3 5.5 collective-permute-start.26
  491.2 5.5 collective-permute-start.31
  509.8 8.9 %collective-permute-start.32 = (f32[128,1,1024]{2,0,1:T(8,128)S(1)}, f32[128,1,1024]{2,0,1:T(8,128)S(1)}, u32[]{:S(2)}, u32[]{:S(2)}) collective-permute-start(f32[128,1,1024]{2,0,1:T(8,128)S(1)} %get-tuple-element.20), channel_id=1, source_target_pairs={{0,8},{8,16},{16,24},{1,9},{9,17},{17,25},{2,10},{10,18},{18,26},{... | collective-permute-start | bytes 1572872 | tf_op jit(solution)/shard_map/ppermute | solution.py:17
  517.2 7.2 %collective-permute-start.33 = (f32[128,1,1024]{2,0,1:T(8,128)S(1)}, f32[128,1,1024]{2,0,1:T(8,128)S(1)}, u32[]{:S(2)}, u32[]{:S(2)}) collective-permute-start(f32[128,1,1024]{2,0,1:T(8,128)S(1)} %get-tuple-element.19), channel_id=1, source_target_pairs={{8,0},{16,8},{24,16},{9,1},{17,9},{25,17},{10,2},{18,10},{26,18},{... | collective-permute-start | bytes 1572872 | tf_op jit(solution)/shard_map/ppermute | solution.py:18
  524.4 5.4 collective-permute-start.35
  528.3 5.6 collective-permute-start.34
  546.1 9.3 %collective-permute-start.36 = (f32[128,1,1024]{2,0,1:T(8,128)S(1)}, f32[128,1,1024]{2,0,1:T(8,128)S(1)}, u32[]{:S(2)}, u32[]{:S(2)}) collective-permute-start(f32[128,1,1024]{2,0,1:T(8,128)S(1)} %get-tuple-element.18), channel_id=1, source_target_pairs={{0,8},{8,16},{16,24},{1,9},{9,17},{17,25},{2,10},{10,18},{18,26},{... | collective-permute-start | bytes 1572872 | tf_op jit(solution)/shard_map/ppermute | solution.py:17
  558.5 4.9 collective-permute-start.39
  561.9 5.6 collective-permute-start.38
  (38 other events, 389.4 us)
where the time goes:
time: 658 us; the launch traced here: 647 us
  blocking collectives  209 us (32%)
  local copies, waits for them, and re-layouts  171 us (26%)
  starting transfers between devices  110 us (17%)
  other arithmetic  74.5 us (11%)
  waiting for transfers between devices  61.1 us (9%)
  matrix products  18.5 us (3%)
    all_to_all x4, blocking collectives, lines_along_x(): return lax.all_to_all(solved, 'px', split_axis=0, concat_axis=2, tiled=True)  84.5 us
    ppermute x20, starting transfers between devices, with_halo(): before = lax.ppermute(last, axis, up)  83.5 us
    all_to_all x4, blocking collectives, lines_along_x(): piece = lax.all_to_all(field, 'px', split_axis=2, concat_axis=0, tiled=True)  80.9 us
    ppermute x20, waiting for transfers between devices, with_halo(): after = lax.ppermute(initial, axis, down)  56.3 us
    slice x8, local copies, waits for them, and re-layouts, take(): lax.slice_in_dim(padded, start, start + length - 1, stride=2, axis=axis)  44.9 us
    unnamed x1, blocking collectives  44 us
    reduce_sum x1, local copies, waits for them, and re-layouts, coarsen(): density.reshape(first // 2, 2, second // 2, 2, third // 2, 2)  35.6 us
    ppermute x20, starting transfers between devices, with_halo(): after = lax.ppermute(initial, axis, down)  26.4 us
  transfers between devices with their start and end apart: 40, of which 24 were waited for; matrix products, arithmetic and copies ran while one was open for 10% of the time, Pallas kernels for 0%

commit v1 on v0

v1 whole, which is shorter than its diff:
```python
import functools

import jax
import jax.numpy as jnp
from jax import lax
from jax.experimental import pallas as pl
from jax.experimental.pallas import tpu as pltpu
from jax.sharding import PartitionSpec as P

f32 = jnp.float32
bf16 = jnp.bfloat16
MESH = pl.DeviceIdType.MESH
shift_term = 0.1
H = 8


def split(a):
    hi = a.astype(bf16)
    return hi, (a - hi.astype(f32)).astype(bf16)


def mm(a, b, transposed=False):
    dims = (((1,), (1 if transposed else 0,)), ((), ()))
    return lax.dot_general(a, b, dims, preferred_element_type=f32)


def mm3(a, b, transposed=False):
    (ah, al), (bh, bl) = a, b
    return mm(ah, bh, transposed) + (mm(ah, bl, transposed) + mm(al, bh, transposed))


def weights(shape, fine_dim, fine_pad, coarse_pad, inner, outer):
    fine = lax.broadcasted_iota(jnp.int32, shape, fine_dim) - fine_pad
    coarse = lax.broadcasted_iota(jnp.int32, shape, 1 - fine_dim) - coarse_pad
    d = fine - 2 * coarse
    near = jnp.where((d == 0) | (d == 1), inner, 0.0)
    if outer:
        near = jnp.where((d == -1) | (d == 2), outer, near)
    return near.astype(bf16)


def left_mul(m, v):
    hi, lo = split(v)
    return mm(m, hi) + mm(m, lo)


def right_mul(v, m):
    hi, lo = split(v)
    return mm(hi, m) + mm(lo, m)


def kernel(
    dims,
    f_in, rho_in, sx_ref, sy_ref, sz_ref, lz0_ref, lx0_in, lz1_ref, lx1_in, c_ref,
    out_ref,
    F, RHO, RD, UA, UB, UC, UD, W, W2, R0, T1, F1, RHO1, RD1,
    M1, M2, MP, M3, M4, V, V2, G1, G2, CB, CX, CX1, CZ1, LX0, LX1, OUT,
    ss, rs, ls,
):
    n, ny, nz, B, npx, npy = dims
    n1, ny1, nz1 = n // 2, ny // 2, nz // 2
    nk, nk1 = nz // B, nz1 // B
    g, g1 = B // n, B // n1
    i, j = lax.axis_index("px"), lax.axis_index("py")
    has_xm, has_xp = i > 0, i < npx - 1
    has_ym, has_yp = j > 0, j < npy - 1
    xm, xp = lax.rem(i + npx - 1, npx), lax.rem(i + 1, npx)
    ym, yp = lax.rem(j + npy - 1, npy), lax.rem(j + 1, npy)

    loads = []
    for y in range(ny):
        loads.append(pltpu.make_async_copy(f_in.at[:, y, :], F.at[y], ls.at[2 * y]))
        loads.append(pltpu.make_async_copy(rho_in.at[:, y, :], RHO.at[y], ls.at[2 * y + 1]))
    at0 = pl.multiple_of(lax.rem(i, g) * n, n)
    at1 = pl.multiple_of(lax.rem(i, g1) * n1, n1)
    loads.append(pltpu.make_async_copy(lx0_in.at[i // g, pl.ds(at0, n), :], LX0, ls.at[2 * ny]))
    loads.append(pltpu.make_async_copy(lx1_in.at[i // g1, pl.ds(at1, n1), :], LX1, ls.at[2 * ny + 1]))
    for load in loads:
        load.start()

    for ref in (UA, UB, UD, R0, M1, M2, M3, M4):
        rows = ref.shape[1]

        @pl.when(jnp.logical_not(has_xm))
        def _(ref=ref):
            ref[:, 0:H, :] = jnp.zeros((ref.shape[0], H, ref.shape[2]), f32)

        @pl.when(jnp.logical_not(has_xp))
        def _(ref=ref, rows=rows):
            ref[:, rows - H:rows, :] = jnp.zeros((ref.shape[0], H, ref.shape[2]), f32)

    for ref in (UA, UB, UD, T1, M1, M2, M3, M4):
        planes = ref.shape[0]

        @pl.when(jnp.logical_not(has_ym))
        def _(ref=ref):
            ref[0] = jnp.zeros(ref.shape[1:], f32)

        @pl.when(jnp.logical_not(has_yp))
        def _(ref=ref, planes=planes):
            ref[planes - 1] = jnp.zeros(ref.shape[1:], f32)

    count = c_ref.shape[1]
    CB[...] = jnp.zeros(CB.shape, f32)
    CB[0, :, 0:count] = jnp.broadcast_to(c_ref[...], (8, count))

    barrier = pltpu.get_barrier_semaphore()
    for s in range(1, npx):
        pl.semaphore_signal(barrier, inc=1, device_id={"px": lax.rem(i + s, npx), "py": j}, device_id_type=MESH)
    for s in range(1, npy):
        pl.semaphore_signal(barrier, inc=1, device_id={"px": i, "py": lax.rem(j + s, npy)}, device_id_type=MESH)
    for to_x in (xm, xp):
        for to_y in (ym, yp):
            pl.semaphore_signal(barrier, inc=1, device_id={"px": to_x, "py": to_y}, device_id_type=MESH)

    pending = []

    def push(src, dst, to_x, to_y, sends=None, receives=None):
        at = len(pending)
        copy = pltpu.make_async_remote_copy(
            src_ref=src, dst_ref=dst, send_sem=ss.at[at], recv_sem=rs.at[at],
            device_id={"px": to_x, "py": to_y}, device_id_type=MESH,
        )
        if sends is None:
            copy.start()
        else:
            pl.when(sends)(copy.start)
        pending.append((sends, copy))
        return receives, copy

    def arrive(handles):
        for receives, copy in handles:
            if receives is None:
                copy.wait_recv()
            else:
                pl.when(receives)(copy.wait_recv)

    def halo_x(ref, planes, rows, zs):
        a, b = planes
        return [
            push(ref.at[a:b, rows:rows + H, zs], ref.at[a:b, 0:H, zs], xp, j, has_xp, has_xm),
            push(ref.at[a:b, H:2 * H, zs], ref.at[a:b, rows + H:rows + 2 * H, zs], xm, j, has_xm, has_xp),
        ]

    def halo_y(ref, planes, r, zs):
        return [
            push(ref.at[planes, r, zs], ref.at[0, r, zs], i, yp, has_yp, has_ym),
            push(ref.at[1, r, zs], ref.at[planes + 1, r, zs], i, ym, has_ym, has_yp),
        ]

    def halo(ref, planes, rows, zs):
        return halo_y(ref, planes, slice(H, H + rows), zs) + halo_x(ref, (1, planes + 1), rows, zs)

    def halo_corners(ref, planes, rows):
        both = jnp.logical_and
        low, high = slice(0, H), slice(rows + H, rows + 2 * H)
        first, last = slice(H, 2 * H), slice(rows, rows + H)
        return [
            push(ref.at[planes, last, :], ref.at[0, low, :], xp, yp, both(has_xp, has_yp), both(has_xm, has_ym)),
            push(ref.at[1, last, :], ref.at[planes + 1, low, :], xp, ym, both(has_xp, has_ym), both(has_xm, has_yp)),
            push(ref.at[planes, first, :], ref.at[0, high, :], xm, yp, both(has_xm, has_yp), both(has_xp, has_ym)),
            push(ref.at[1, first, :], ref.at[planes + 1, high, :], xm, ym, both(has_xm, has_ym), both(has_xp, has_yp)),
        ]

    def to_block(ref, at, rows, peers, zs):
        here = lax.rem(i, peers)
        base = i - here
        mine = ref.at[:, pl.ds(at, rows), zs]
        return [push(mine, mine, base + lax.rem(here + s, peers), j) for s in range(1, peers)]

    def residual(rhs, ref, rho, cx, cys, cz, y, k):
        rows = rhs.shape[1]
        lo = k * B
        zs = slice(lo, lo + B)
        own = slice(H, H + rows)
        c = ref[y + 1, own, zs]
        near_x = ref[y + 1, H - 1:H - 1 + rows, zs] + ref[y + 1, H + 1:H + 1 + rows, zs]
        near_y = ref[y, own, zs] + ref[y + 2, own, zs]
        blank = jnp.zeros((rows, 128), f32)
        left = ref[y + 1, own, lo - 128:lo] if lo > 0 else blank
        right = ref[y + 1, own, lo + B:lo + B + 128] if lo + B < ref.shape[2] else blank
        wide = jnp.concatenate([left, c, right], axis=1)
        near_z = (pltpu.roll(wide, 1, 1) + pltpu.roll(wide, B + 255, 1))[:, 128:128 + B]
        twice = 2.0 * c
        stencil = cx[...] * (twice - near_x) + cys[y] * (twice - near_y) + cz[0:1, zs] * (twice - near_z)
        return rhs[y, :, zs] - (shift_term * c + rho[y, :, zs] * stencil)

    def inverse_diagonal(rho, cx, cys, cz, y, k):
        zs = slice(k * B, k * B + B)
        return 1.0 / (shift_term + 2.0 * rho[y, :, zs] * (cx[...] + cys[y] + cz[0:1, zs]))

    square = (n, n)
    diag = lax.broadcasted_iota(jnp.int32, square, 0) == lax.broadcasted_iota(jnp.int32, square, 1)
    column = jnp.sum(jnp.where(diag, jnp.broadcast_to(sx_ref[...], square), 0.0), axis=1, keepdims=True)
    CX[...] = jnp.broadcast_to(column, (n, B))
    cy = [sy_ref[y] for y in range(ny)]
    cy1 = [(cy[2 * y] + cy[2 * y + 1]) * 0.125 for y in range(ny1)]

    for load in loads:
        load.wait()
    pl.semaphore_wait(barrier, npx + npy + 2)

    whole = slice(None)
    neighbours = [
        push(CB.at[0], CB.at[1], xp, j, has_xp, has_xm),
        push(CB.at[0], CB.at[2], xm, j, has_xm, has_xp),
        push(CB.at[0], CB.at[3], i, yp, has_yp, has_ym),
        push(CB.at[0], CB.at[4], i, ym, has_ym, has_yp),
    ]

    def smooth_z(values, block, planes, rows):
        w = jnp.concatenate(values, axis=0)
        z = mm3(split(w), split(block), True)
        return [z[y * rows:(y + 1) * rows] for y in range(planes)]

    own = slice(H, H + n)
    halos = []
    for k in range(nk):
        zs = slice(k * B, k * B + B)
        scaled = []
        for y in range(ny):
            rd = inverse_diagonal(RHO, CX, cy, sz_ref, y, k)
            RD[y, :, zs] = rd
            scaled.append(F[y, :, zs] * rd)
        solved = smooth_z(scaled, lz0_ref[k], ny, n)
        for y in range(ny):
            UA[y + 1, own, zs] = solved[y]
        halos.append(halo(UA, ny, n, zs))

    def exchange_fine(ref, halos, target):
        blocks = []
        for k in range(nk):
            zs = slice(k * B, k * B + B)
            arrive(halos[k])
            for y in range(ny):
                r = residual(F, ref, RHO, CX, cy, sz_ref, y, k)
                target[y, pl.ds(at0, n), zs] = r * RD[y, :, zs]
            blocks.append(to_block(target, at0, n, g, zs))
        return blocks

    blocks = exchange_fine(UA, halos, W)

    restrict_x = weights((n1, n + 2 * H), 1, H, 0, 0.375, 0.125)
    restrict_z = weights((nz, nz1), 0, 0, 0, 0.375, 0.125)
    mean_x = weights((n1, n), 1, 0, 0, 0.5, 0.0)
    mean_z = weights((nz, nz1), 0, 0, 0, 0.5, 0.0)
    CX1[...] = left_mul(mean_x, CX[...]) * 0.25
    CZ1[...] = right_mul(jnp.broadcast_to(sz_ref[...], (8, nz)), mean_z) * 0.25
    for y in range(ny1):
        pair = (RHO[2 * y] + RHO[2 * y + 1]) * 0.5
        RHO1[y] = right_mul(left_mul(mean_x, pair), mean_z)
    for y in range(ny1):
        for k in range(nk1):
            RD1[y, :, k * B:k * B + B] = inverse_diagonal(RHO1, CX1, cy1, CZ1, y, k)

    lx0 = split(LX0[...])
    halos = []
    for k in range(nk):
        zs = slice(k * B, k * B + B)
        arrive(blocks[k])
        for y in range(ny):
            UB[y + 1, own, zs] = UA[y + 1, own, zs] + mm3(lx0, split(W[y, :, zs]))
        halos.append(halo(UB, ny, n, zs))

    for k in range(nk):
        zs = slice(k * B, k * B + B)
        arrive(halos[k])
        for y in range(ny):
            R0[y, own, zs] = residual(F, UB, RHO, CX, cy, sz_ref, y, k)
    arrive(halo_x(R0, (0, ny), n, whole))
    for y in range(ny):
        T1[y + 1] = right_mul(left_mul(restrict_x, R0[y]), restrict_z)
    arrive(halo_y(T1, ny, whole, whole))
    for y in range(ny1):
        a = 2 * y
        F1[y] = (T1[a] + 3.0 * T1[a + 1] + 3.0 * T1[a + 2] + T1[a + 3]) * 0.125

    own1 = slice(H, H + n1)

    def middle_z(ref, before, rhs):
        for k in range(nk1):
            zs = slice(k * B, k * B + B)
            solved = smooth_z([r * RD1[y, :, zs] for y, r in enumerate(rhs(k))], lz1_ref[k], ny1, n1)
            for y in range(ny1):
                ref[y + 1, own1, zs] = solved[y] if before is None else before[y + 1, own1, zs] + solved[y]
        return halo(ref, ny1, n1, whole)

    def middle_x(ref, target, result):
        for k in range(nk1):
            zs = slice(k * B, k * B + B)
            for y in range(ny1):
                r = residual(F1, ref, RHO1, CX1, cy1, CZ1, y, k)
                target[y, pl.ds(at1, n1), zs] = r * RD1[y, :, zs]
        arrive(to_block(target, at1, n1, g1, whole))
        lx1 = split(LX1[...])
        for y in range(ny1):
            result[y + 1, own1, :] = ref[y + 1, own1, :] + mm3(lx1, split(target[y]))

    arrive(middle_z(M1, None, lambda k: [F1[y, :, k * B:k * B + B] for y in range(ny1)]))
    middle_x(M1, V, M2)
    arrive(halo(M2, ny1, n1, whole))

    total = jnp.zeros((1, B), f32)
    for y in range(ny1):
        for k in range(nk1):
            r = residual(F1, M2, RHO1, CX1, cy1, CZ1, y, k)
            total = total + jnp.sum(r, axis=0, keepdims=True)
    mean = jnp.sum(total, axis=1, keepdims=True) * (1.0 / (ny1 * n1 * nz1))
    lane = lax.broadcasted_iota(jnp.int32, CB.shape[1:], 1)
    G1[i] = jnp.where(lane == j * npx + i, mean, 0.0)
    arrive([push(G1.at[i], G1.at[i], lax.rem(i + s, npx), j) for s in range(1, npx)])
    G2[j] = jnp.sum(G1[...], axis=0)
    arrive([push(G2.at[j], G2.at[j], i, lax.rem(j + s, npy)) for s in range(1, npy)])
    means = jnp.sum(G2[...], axis=0)[0:1]
    arrive(neighbours)
    e = [jnp.sum(CB[s][0:1] * means, axis=1, keepdims=True) for s in range(5)]
    MP[1:ny1 + 1, own1, :] = M2[1:ny1 + 1, own1, :] + e[0]
    MP[1:ny1 + 1, 0:H, :] = M2[1:ny1 + 1, 0:H, :] + e[1]
    MP[1:ny1 + 1, n1 + H:n1 + 2 * H, :] = M2[1:ny1 + 1, n1 + H:n1 + 2 * H, :] + e[2]
    MP[0, own1, :] = M2[0, own1, :] + e[3]
    MP[ny1 + 1, own1, :] = M2[ny1 + 1, own1, :] + e[4]

    arrive(middle_z(M3, MP, lambda k: [residual(F1, MP, RHO1, CX1, cy1, CZ1, y, k) for y in range(ny1)]))
    middle_x(M3, V2, M4)
    handles = halo(M4, ny1, n1, whole) + halo_corners(M4, ny1, n1)
    raise_x = weights((n + 2 * H, n1 + 2 * H), 0, H, H, 0.75, 0.25)
    raise_z = weights((nz1, nz), 1, 0, 0, 0.75, 0.25)
    arrive(handles)

    raised = [left_mul(raise_x, right_mul(M4[y], raise_z)) for y in range(ny1 + 2)]
    row = lax.broadcasted_iota(jnp.int32, (n + 2 * H, 1), 0)
    inside = jnp.logical_and(jnp.logical_or(row >= H, has_xm), jnp.logical_or(row < n + H, has_xp))
    for y in range(ny + 2):
        near = (y - 1) // 2 + 1
        other = near - 1 if (y - 1) % 2 == 0 else near + 1
        c = (3.0 * raised[near] + raised[other]) * 0.25
        if y == 0:
            UC[0, own, :] = jnp.where(has_ym, UB[0, own, :] + c[own], 0.0)
        elif y == ny + 1:
            UC[y, own, :] = jnp.where(has_yp, UB[y, own, :] + c[own], 0.0)
        else:
            UC[y] = jnp.where(inside, UB[y] + c, 0.0)

    halos = []
    for k in range(nk):
        zs = slice(k * B, k * B + B)
        scaled = [residual(F, UC, RHO, CX, cy, sz_ref, y, k) * RD[y, :, zs] for y in range(ny)]
        solved = smooth_z(scaled, lz0_ref[k], ny, n)
        for y in range(ny):
            UD[y + 1, own, zs] = UC[y + 1, own, zs] + solved[y]
        halos.append(halo(UD, ny, n, zs))
    blocks = exchange_fine(UD, halos, W2)
    lx0 = split(LX0[...])
    for k in range(nk):
        zs = slice(k * B, k * B + B)
        arrive(blocks[k])
        for y in range(ny):
            OUT[y, :, zs] = UD[y + 1, own, zs] + mm3(lx0, split(W2[y, :, zs]))
    stores = [pltpu.make_async_copy(OUT.at[y], out_ref.at[:, y, :], ls.at[y]) for y in range(ny)]
    for store in stores:
        store.start()
    for sends, copy in pending:
        if sends is None:
            copy.wait_send()
        else:
            pl.when(sends)(copy.wait_send)
    for store in stores:
        store.wait()


def per_device(npx, npy, f, rho, sx, sy, sz, lz0, lx0, lz1, lx1, c):
    n, ny, nz = f.shape
    B = lz0.shape[-1]
    n1, ny1, nz1 = n // 2, ny // 2, nz // 2
    g, g1, nk = B // n, B // n1, nz // B
    lanes = -(-c.shape[1] // 128) * 128
    fine = pltpu.VMEM((ny, n, nz), f32)
    padded = pltpu.VMEM((ny + 2, n + 2 * H, nz), f32)
    coarse = pltpu.VMEM((ny1, n1, nz1), f32)
    coarse_padded = pltpu.VMEM((ny1 + 2, n1 + 2 * H, nz1), f32)
    copies = 4 + 12 * nk + 2 * nk * (g - 1) + 4 + 4 * 4 + 4 + 2 * (g1 - 1) + npx + npy - 2
    anywhere = pl.BlockSpec(memory_space=pl.ANY)
    vmem = pl.BlockSpec(memory_space=pltpu.VMEM)
    smem = pl.BlockSpec(memory_space=pltpu.SMEM)
    return pl.pallas_call(
        functools.partial(kernel, (n, ny, nz, B, npx, npy)),
        out_shape=jax.ShapeDtypeStruct(f.shape, f32),
        in_specs=[anywhere, anywhere, vmem, smem, vmem, vmem, anywhere, vmem, anywhere, vmem],
        out_specs=anywhere,
        scratch_shapes=[
            fine, fine, fine, padded, padded, padded, padded,
            pltpu.VMEM((ny, B, nz), f32), pltpu.VMEM((ny, B, nz), f32),
            pltpu.VMEM((ny, n + 2 * H, nz), f32), pltpu.VMEM((ny + 2, n1, nz1), f32),
            coarse, coarse, coarse,
            coarse_padded, coarse_padded, coarse_padded, coarse_padded, coarse_padded,
            pltpu.VMEM((ny1, B, nz1), f32), pltpu.VMEM((ny1, B, nz1), f32),
            pltpu.VMEM((npx, 8, lanes), f32), pltpu.VMEM((npy, 8, lanes), f32), pltpu.VMEM((5, 8, lanes), f32),
            pltpu.VMEM((n, B), f32), pltpu.VMEM((n1, B), f32), pltpu.VMEM((8, nz1), f32),
            pltpu.VMEM((n, B), f32), pltpu.VMEM((n1, B), f32), fine,
            pltpu.SemaphoreType.DMA((copies,)), pltpu.SemaphoreType.DMA((copies,)),
            pltpu.SemaphoreType.DMA((2 * ny + 2,)),
        ],
        compiler_params=pltpu.CompilerParams(
            collective_id=0, has_side_effects=True, vmem_limit_bytes=56 * 1024 * 1024
        ),
    )(f, rho, sx.reshape(1, n), sy, sz.reshape(1, nz), lz0, lx0, lz1, lx1, c)


def solution(mesh):
    placed = (
        P("px", "py", None), P("px", "py", None), P("px"), P("py"),
        P(), P(), P(), P(), P(), P(("py", "px"), None),
    )
    body = functools.partial(per_device, mesh.shape["px"], mesh.shape["py"])
    return jax.shard_map(
        body, mesh=mesh, in_specs=placed, out_specs=P("px", "py", None), check_vma=False
    )
```

time: 658 us -> 122 us (0.19); the launches traced: 647 us -> 121 us
  blocking collectives: 209 us -> 0 us
  local copies, waits for them, and re-layouts: 171 us -> 2.26 us
  Pallas kernels: 0 us -> 119 us
  starting transfers between devices: 110 us -> 0 us
  other arithmetic: 74.5 us -> 0 us
  waiting for transfers between devices: 61.1 us -> 0 us
  matrix products: 18.5 us -> 0 us
    all_to_all x8 -> x0, blocking collectives: 165 us -> none  [the longest x4 84.5 us: lines_along_x(): return lax.all_to_all(solved, 'px', split_axis=0, concat_axis=2, tiled=True)]
    pallas_call x0 -> x1, Pallas kernels: none -> 119 us  [per_device(): pl.pallas_call(functools.partial(kernel, (n, ny, nz, B, npx, npy)), out_s...]
    ppermute x40 -> x0, starting transfers between devices: 110 us -> none  [the longest x20 83.5 us: with_halo(): before = lax.ppermute(last, axis, up)]
    ppermute x40 -> x0, waiting for transfers between devices: 61.1 us -> none  [the longest x20 56.3 us: with_halo(): after = lax.ppermute(initial, axis, down)]
    slice x17 -> x0, local copies, waits for them, and re-layouts: 46.4 us -> none  [the longest x8 44.9 us: take(): lax.slice_in_dim(padded, start, start + length - 1, stride=2, axis=axis)]
    unnamed x1 -> x0, blocking collectives: 44 us -> none
    reduce_sum x1 -> x0, local copies, waits for them, and re-layouts: 35.6 us -> none  [coarsen(): density.reshape(first // 2, 2, second // 2, 2, third // 2, 2)]
    reshape x21 -> x0, local copies, waits for them, and re-layouts: 31.3 us -> none  [the longest x4 7.29 us: lines_along_x(): grouped = piece.reshape(count, rows // count, items * depth)]
  transfers between devices with their start and end apart: 40 -> 0, of which waited for: 24 -> 0; matrix products, arithmetic and copies ran while one was open for 10% -> 0% of each run, Pallas kernels for 0% -> 0%
where the time goes in v1:
time: 122 us; the launch traced here: 121 us
  Pallas kernels  119 us (98%)
  local copies, waits for them, and re-layouts  2.26 us (2%)
    pallas_call x1, Pallas kernels, per_device(): pl.pallas_call(functools.partial(kernel, (n, ny, nz, B, npx, npy)), out_s...  119 us

profile of v1, /device:TPU:0, one launch (start us, length us, event | category | flops | bytes accessed | tf_op | source)
XLA Modules:
  0.0 121.4 jit_solution(5056795267425412784)
XLA Ops:
  0.0 119.1 %shard_map.100 = f32[128,2,1024]{2,1,0:T(2,128)} custom-call(f32[128,2,1024]{2,1,0:T(2,128)} %f_in.1, f32[128,2,1024]{2,1,0:T(2,128)} %rho_in.1, f32[1,128]{1,0:T(1,128)} %bitcast.3, f32[2]{0:T(128)} %sy_ref.1, f32[1,1024]{1,0:T(1,128)} %bitcast.2, f32[4,256,256]{2,1,0:T(8,128)} %lz0_ref.1, f32[4,256,256]{2,1,0:T(8,128)} %lx0_in.1, f32[2,256,256]{2,1,0:T(8,128)} %lz1_ref.1, ...), custom_call_target="tpu_custom_call" | custom-call | tf_op jit(solution)/shard_map/pallas_call | solution.py:385
  119.1 2.3 %copy.12 = f32[128,2,1024]{2,1,0:T(2,128)} copy(f32[128,2,1024]{2,1,0:T(2,128)} %shard_map.100) | data formatting | bytes 2097152

commit v2 on v1

--- a/solution.py
+++ b/solution.py
@@ -51,10 +51,10 @@
 
 def kernel(
     dims,
-    f_in, rho_in, sx_ref, sy_ref, sz_ref, lz0_ref, lx0_in, lz1_ref, lx1_in, c_ref,
+    f_in, rho_in, sx_ref, sy_ref, sz_ref, lz0_in, lx0_in, lz1_in, lx1_in, c_ref,
     out_ref,
-    F, RHO, RD, UA, UB, UC, UD, W, W2, R0, T1, F1, RHO1, RD1,
-    M1, M2, MP, M3, M4, V, V2, G1, G2, CB, CX, CX1, CZ1, LX0, LX1, OUT,
+    F, RHO, RD, UA, UB, UC, UD, W, W2, R0, TX, T1, F1, RHO1, RD1,
+    M1, M2, MP, M3, M4, V, V2, G1, G2, CB, CX, CX1, CZ1, LZ0, LZ1, LX0, LX1, OUT,
     ss, rs, ls,
 ):
     n, ny, nz, B, npx, npy = dims
@@ -68,15 +68,29 @@
     ym, yp = lax.rem(j + npy - 1, npy), lax.rem(j + 1, npy)
 
     loads = []
-    for y in range(ny):
-        loads.append(pltpu.make_async_copy(f_in.at[:, y, :], F.at[y], ls.at[2 * y]))
-        loads.append(pltpu.make_async_copy(rho_in.at[:, y, :], RHO.at[y], ls.at[2 * y + 1]))
+
+    def load(src, dst):
+        copy = pltpu.make_async_copy(src, dst, ls.at[len(loads)])
+        copy.start()
+        loads.append(copy)
+        return copy
+
+    half = B // 2
+    cols = [slice(k * B, k * B + B) for k in range(nk)]
+    parts = []
+    for k in range(nk):
+        part = [load(lz0_in.at[k], LZ0.at[k])]
+        for y in range(ny):
+            part.append(load(f_in.at[:, y, cols[k]], F.at[y, :, cols[k]]))
+            part.append(load(rho_in.at[:, y, cols[k]], RHO.at[y, :, cols[k]]))
+        parts.append(part)
     at0 = pl.multiple_of(lax.rem(i, g) * n, n)
     at1 = pl.multiple_of(lax.rem(i, g1) * n1, n1)
-    loads.append(pltpu.make_async_copy(lx0_in.at[i // g, pl.ds(at0, n), :], LX0, ls.at[2 * ny]))
-    loads.append(pltpu.make_async_copy(lx1_in.at[i // g1, pl.ds(at1, n1), :], LX1, ls.at[2 * ny + 1]))
-    for load in loads:
-        load.start()
+    late = [
+        load(lx0_in.at[i // g, pl.ds(at0, n), :], LX0),
+        load(lx1_in.at[i // g1, pl.ds(at1, n1), :], LX1),
+        load(lz1_in, LZ1),
+    ]
 
     for ref in (UA, UB, UD, R0, M1, M2, M3, M4):
         rows = ref.shape[1]
@@ -151,15 +165,15 @@
     def halo(ref, planes, rows, zs):
         return halo_y(ref, planes, slice(H, H + rows), zs) + halo_x(ref, (1, planes + 1), rows, zs)
 
-    def halo_corners(ref, planes, rows):
+    def halo_corners(ref, planes, rows, zs):
         both = jnp.logical_and
         low, high = slice(0, H), slice(rows + H, rows + 2 * H)
         first, last = slice(H, 2 * H), slice(rows, rows + H)
         return [
-            push(ref.at[planes, last, :], ref.at[0, low, :], xp, yp, both(has_xp, has_yp), both(has_xm, has_ym)),
-            push(ref.at[1, last, :], ref.at[planes + 1, low, :], xp, ym, both(has_xp, has_ym), both(has_xm, has_yp)),
-            push(ref.at[planes, first, :], ref.at[0, high, :], xm, yp, both(has_xm, has_yp), both(has_xp, has_ym)),
-            push(ref.at[1, first, :], ref.at[planes + 1, high, :], xm, ym, both(has_xm, has_ym), both(has_xp, has_yp)),
+            push(ref.at[planes, last, zs], ref.at[0, low, zs], xp, yp, both(has_xp, has_yp), both(has_xm, has_ym)),
+            push(ref.at[1, last, zs], ref.at[planes + 1, low, zs], xp, ym, both(has_xp, has_ym), both(has_xm, has_yp)),
+            push(ref.at[planes, first, zs], ref.at[0, high, zs], xm, yp, both(has_xm, has_yp), both(has_xp, has_ym)),
+            push(ref.at[1, first, zs], ref.at[planes + 1, high, zs], xm, ym, both(has_xm, has_ym), both(has_xp, has_yp)),
         ]
 
     def to_block(ref, at, rows, peers, zs):
@@ -196,113 +210,162 @@
     cy = [sy_ref[y] for y in range(ny)]
     cy1 = [(cy[2 * y] + cy[2 * y + 1]) * 0.125 for y in range(ny1)]
 
-    for load in loads:
-        load.wait()
-    pl.semaphore_wait(barrier, npx + npy + 2)
-
-    whole = slice(None)
-    neighbours = [
-        push(CB.at[0], CB.at[1], xp, j, has_xp, has_xm),
-        push(CB.at[0], CB.at[2], xm, j, has_xm, has_xp),
-        push(CB.at[0], CB.at[3], i, yp, has_yp, has_ym),
-        push(CB.at[0], CB.at[4], i, ym, has_ym, has_yp),
-    ]
+    neighbours = []
+
+    def enter():
+        pl.semaphore_wait(barrier, npx + npy + 2)
+        neighbours.extend([
+            push(CB.at[0], CB.at[1], xp, j, has_xp, has_xm),
+            push(CB.at[0], CB.at[2], xm, j, has_xm, has_xp),
+            push(CB.at[0], CB.at[3], i, yp, has_yp, has_ym),
+            push(CB.at[0], CB.at[4], i, ym, has_ym, has_yp),
+        ])
 
     def smooth_z(values, block, planes, rows):
         w = jnp.concatenate(values, axis=0)
         z = mm3(split(w), split(block), True)
         return [z[y * rows:(y + 1) * rows] for y in range(planes)]
 
+    def window(ref, y, k, width, side):
+        lo = k * width
+        parts = [ref[y, :, lo:lo + width]]
+        blank = jnp.zeros((ref.shape[1], side), f32)
+        parts.insert(0, ref[y, :, lo - side:lo] if lo > 0 else blank)
+        parts.append(ref[y, :, lo + width:lo + width + side] if lo + width < ref.shape[2] else blank)
+        return jnp.concatenate(parts, axis=1)
+
     own = slice(H, H + n)
-    halos = []
+    own1 = slice(H, H + n1)
+    mean_x = weights((n1, n), 1, 0, 0, 0.5, 0.0)
+    mean_z = weights((B, half), 0, 0, 0, 0.5, 0.0)
+
+    def scaled_residual(ref, halos, target, blocks, k):
+        arrive(halos[k])
+        for y in range(ny):
+            r = residual(F, ref, RHO, CX, cy, sz_ref, y, k)
+            target[y, pl.ds(at0, n), cols[k]] = r * RD[y, :, cols[k]]
+        blocks.append(to_block(target, at0, n, g, cols[k]))
+
+    halos, blocks = [], []
+    for k in range(nk + 1):
+        if k < nk:
+            for copy in parts[k]:
+                copy.wait()
+            scaled = []
+            for y in range(ny):
+                rd = inverse_diagonal(RHO, CX, cy, sz_ref, y, k)
+                RD[y, :, cols[k]] = rd
+                scaled.append(F[y, :, cols[k]] * rd)
+            solved = smooth_z(scaled, LZ0[k], ny, n)
+            for y in range(ny):
+                UA[y + 1, own, cols[k]] = solved[y]
+            if k == 0:
+                enter()
+            halos.append(halo(UA, ny, n, cols[k]))
+        if k > 0:
+            scaled_residual(UA, halos, W, blocks, k - 1)
+
+    for copy in late:
+        copy.wait()
+    restrict_x = weights((n1, n + 2 * H), 1, H, 0, 0.375, 0.125)
+    restrict_z = weights((B + 256, half), 0, 128, 0, 0.375, 0.125)
+    CX1[...] = left_mul(mean_x, CX[...]) * 0.25
     for k in range(nk):
-        zs = slice(k * B, k * B + B)
-        scaled = []
-        for y in range(ny):
-            rd = inverse_diagonal(RHO, CX, cy, sz_ref, y, k)
-            RD[y, :, zs] = rd
-            scaled.append(F[y, :, zs] * rd)
-        solved = smooth_z(scaled, lz0_ref[k], ny, n)
-        for y in range(ny):
-            UA[y + 1, own, zs] = solved[y]
-        halos.append(halo(UA, ny, n, zs))
-
-    def exchange_fine(ref, halos, target):
-        blocks = []
-        for k in range(nk):
-            zs = slice(k * B, k * B + B)
-            arrive(halos[k])
-            for y in range(ny):
-                r = residual(F, ref, RHO, CX, cy, sz_ref, y, k)
-                target[y, pl.ds(at0, n), zs] = r * RD[y, :, zs]
-            blocks.append(to_block(target, at0, n, g, zs))
-        return blocks
-
-    blocks = exchange_fine(UA, halos, W)
-
-    restrict_x = weights((n1, n + 2 * H), 1, H, 0, 0.375, 0.125)
-    restrict_z = weights((nz, nz1), 0, 0, 0, 0.375, 0.125)
-    mean_x = weights((n1, n), 1, 0, 0, 0.5, 0.0)
-    mean_z = weights((nz, nz1), 0, 0, 0, 0.5, 0.0)
-    CX1[...] = left_mul(mean_x, CX[...]) * 0.25
-    CZ1[...] = right_mul(jnp.broadcast_to(sz_ref[...], (8, nz)), mean_z) * 0.25
-    for y in range(ny1):
-        pair = (RHO[2 * y] + RHO[2 * y + 1]) * 0.5
-        RHO1[y] = right_mul(left_mul(mean_x, pair), mean_z)
+        fine_z = jnp.broadcast_to(sz_ref[:, cols[k]], (8, B))
+        CZ1[:, k * half:k * half + half] = right_mul(fine_z, mean_z) * 0.25
+        for y in range(ny1):
+            pair = (RHO[2 * y, :, cols[k]] + RHO[2 * y + 1, :, cols[k]]) * 0.5
+            RHO1[y, :, k * half:k * half + half] = right_mul(left_mul(mean_x, pair), mean_z)
     for y in range(ny1):
         for k in range(nk1):
-            RD1[y, :, k * B:k * B + B] = inverse_diagonal(RHO1, CX1, cy1, CZ1, y, k)
+            RD1[y, :, cols[k]] = inverse_diagonal(RHO1, CX1, cy1, CZ1, y, k)
 
     lx0 = split(LX0[...])
-    halos = []
+    halos, rims, sides, halos1 = [], [], [], []
+
+    def fine_residual(k):
+        arrive(halos[k])
+        for y in range(ny):
+            R0[y, own, cols[k]] = residual(F, UB, RHO, CX, cy, sz_ref, y, k)
+        rims.append(halo_x(R0, (0, ny), n, cols[k]))
+
+    def restrict_rows(k):
+        arrive(rims[k])
+        for y in range(ny):
+            TX[y, :, cols[k]] = left_mul(restrict_x, R0[y, :, cols[k]])
+
+    def restrict_columns(k):
+        zs = slice(k * half, k * half + half)
+        for y in range(ny):
+            T1[y + 1, :, zs] = right_mul(window(TX, y, k, B, 128), restrict_z)
+        sides.append(halo_y(T1, ny, slice(None), zs))
+
+    def middle_rhs(k):
+        arrive(sides[2 * k])
+        arrive(sides[2 * k + 1])
+        for y in range(ny1):
+            a = 2 * y
+            inner = T1[a + 1, :, cols[k]] + T1[a + 2, :, cols[k]]
+            F1[y, :, cols[k]] = (T1[a, :, cols[k]] + 3.0 * inner + T1[a + 3, :, cols[k]]) * 0.125
+
+    def middle_z(ref, before, rhs, k):
+        scaled = [r * RD1[y, :, cols[k]] for y, r in enumerate(rhs)]
+        solved = smooth_z(scaled, LZ1[k], ny1, n1)
+        for y in range(ny1):
+            u = solved[y] if before is None else before[y + 1, own1, cols[k]] + solved[y]
+            ref[y + 1, own1, cols[k]] = u
+        return halo(ref, ny1, n1, cols[k])
+
+    def middle_first(k):
+        middle_rhs(k)
+        halos1.append(middle_z(M1, None, [F1[y, :, cols[k]] for y in range(ny1)], k))
+
     for k in range(nk):
-        zs = slice(k * B, k * B + B)
         arrive(blocks[k])
         for y in range(ny):
-            UB[y + 1, own, zs] = UA[y + 1, own, zs] + mm3(lx0, split(W[y, :, zs]))
-        halos.append(halo(UB, ny, n, zs))
-
-    for k in range(nk):
-        zs = slice(k * B, k * B + B)
-        arrive(halos[k])
-        for y in range(ny):
-            R0[y, own, zs] = residual(F, UB, RHO, CX, cy, sz_ref, y, k)
-    arrive(halo_x(R0, (0, ny), n, whole))
-    for y in range(ny):
-        T1[y + 1] = right_mul(left_mul(restrict_x, R0[y]), restrict_z)
-    arrive(halo_y(T1, ny, whole, whole))
-    for y in range(ny1):
-        a = 2 * y
-        F1[y] = (T1[a] + 3.0 * T1[a + 1] + 3.0 * T1[a + 2] + T1[a + 3]) * 0.125
-
-    own1 = slice(H, H + n1)
-
-    def middle_z(ref, before, rhs):
+            UB[y + 1, own, cols[k]] = UA[y + 1, own, cols[k]] + mm3(lx0, split(W[y, :, cols[k]]))
+        halos.append(halo(UB, ny, n, cols[k]))
+        if k >= 1:
+            fine_residual(k - 1)
+            restrict_rows(k - 1)
+        if k >= 2:
+            restrict_columns(k - 2)
+    fine_residual(nk - 1)
+    for k in range(nk1 - 1):
+        middle_first(k)
+    restrict_rows(nk - 1)
+    restrict_columns(nk - 2)
+    restrict_columns(nk - 1)
+    middle_first(nk1 - 1)
+
+    lx1 = split(LX1[...])
+
+    def middle_x(ref, halos1, target, result, diagonals):
+        sent = []
         for k in range(nk1):
-            zs = slice(k * B, k * B + B)
-            solved = smooth_z([r * RD1[y, :, zs] for y, r in enumerate(rhs(k))], lz1_ref[k], ny1, n1)
-            for y in range(ny1):
-                ref[y + 1, own1, zs] = solved[y] if before is None else before[y + 1, own1, zs] + solved[y]
-        return halo(ref, ny1, n1, whole)
-
-    def middle_x(ref, target, result):
-        for k in range(nk1):
-            zs = slice(k * B, k * B + B)
+            arrive(halos1[k])
             for y in range(ny1):
                 r = residual(F1, ref, RHO1, CX1, cy1, CZ1, y, k)
-                target[y, pl.ds(at1, n1), zs] = r * RD1[y, :, zs]
-        arrive(to_block(target, at1, n1, g1, whole))
-        lx1 = split(LX1[...])
+                target[y, pl.ds(at1, n1), cols[k]] = r * RD1[y, :, cols[k]]
+            sent.append(to_block(target, at1, n1, g1, cols[k]))
+        edges = []
+        for k in range(nk1):
+            arrive(sent[k])
+            for y in range(ny1):
+                solved = mm3(lx1, split(target[y, :, cols[k]]))
+                result[y + 1, own1, cols[k]] = ref[y + 1, own1, cols[k]] + solved
+            edge = halo(result, ny1, n1, cols[k])
+            if diagonals:
+                edge = edge + halo_corners(result, ny1, n1, cols[k])
+            edges.append(edge)
+        return edges
+
+    edges = middle_x(M1, halos1, V, M2, False)
+
+    total = jnp.zeros((1, B), f32)
+    for k in range(nk1):
+        arrive(edges[k])
         for y in range(ny1):
-            result[y + 1, own1, :] = ref[y + 1, own1, :] + mm3(lx1, split(target[y]))
-
-    arrive(middle_z(M1, None, lambda k: [F1[y, :, k * B:k * B + B] for y in range(ny1)]))
-    middle_x(M1, V, M2)
-    arrive(halo(M2, ny1, n1, whole))
-
-    total = jnp.zeros((1, B), f32)
-    for y in range(ny1):
-        for k in range(nk1):
             r = residual(F1, M2, RHO1, CX1, cy1, CZ1, y, k)
             total = total + jnp.sum(r, axis=0, keepdims=True)
     mean = jnp.sum(total, axis=1, keepdims=True) * (1.0 / (ny1 * n1 * nz1))
@@ -320,45 +383,57 @@
     MP[0, own1, :] = M2[0, own1, :] + e[3]
     MP[ny1 + 1, own1, :] = M2[ny1 + 1, own1, :] + e[4]
 
-    arrive(middle_z(M3, MP, lambda k: [residual(F1, MP, RHO1, CX1, cy1, CZ1, y, k) for y in range(ny1)]))
-    middle_x(M3, V2, M4)
-    handles = halo(M4, ny1, n1, whole) + halo_corners(M4, ny1, n1)
+    halos1 = []
+    for k in range(nk1):
+        rhs = [residual(F1, MP, RHO1, CX1, cy1, CZ1, y, k) for y in range(ny1)]
+        halos1.append(middle_z(M3, MP, rhs, k))
+    edges = middle_x(M3, halos1, V2, M4, True)
+
     raise_x = weights((n + 2 * H, n1 + 2 * H), 0, H, H, 0.75, 0.25)
-    raise_z = weights((nz1, nz), 1, 0, 0, 0.75, 0.25)
-    arrive(handles)
-
-    raised = [left_mul(raise_x, right_mul(M4[y], raise_z)) for y in range(ny1 + 2)]
+    raise_z = weights((half + 256, B), 1, 0, 128, 0.75, 0.25)
     row = lax.broadcasted_iota(jnp.int32, (n + 2 * H, 1), 0)
     inside = jnp.logical_and(jnp.logical_or(row >= H, has_xm), jnp.logical_or(row < n + H, has_xp))
-    for y in range(ny + 2):
-        near = (y - 1) // 2 + 1
-        other = near - 1 if (y - 1) % 2 == 0 else near + 1
-        c = (3.0 * raised[near] + raised[other]) * 0.25
-        if y == 0:
-            UC[0, own, :] = jnp.where(has_ym, UB[0, own, :] + c[own], 0.0)
-        elif y == ny + 1:
-            UC[y, own, :] = jnp.where(has_yp, UB[y, own, :] + c[own], 0.0)
-        else:
-            UC[y] = jnp.where(inside, UB[y] + c, 0.0)
-
-    halos = []
+    arrived = []
+
+    def prolong(k):
+        while len(arrived) < min(k + 1, nk - 1) // 2 + 1:
+            arrive(edges[len(arrived)])
+            arrived.append(k)
+        zs = cols[k]
+        raised = [left_mul(raise_x, right_mul(window(M4, y, k, half, 128), raise_z)) for y in range(ny1 + 2)]
+        for y in range(ny + 2):
+            near = (y - 1) // 2 + 1
+            other = near - 1 if (y - 1) % 2 == 0 else near + 1
+            c = (3.0 * raised[near] + raised[other]) * 0.25
+            if y == 0:
+                UC[0, own, zs] = jnp.where(has_ym, UB[0, own, zs] + c[own], 0.0)
+            elif y == ny + 1:
+                UC[y, own, zs] = jnp.where(has_yp, UB[y, own, zs] + c[own], 0.0)
+            else:
+                UC[y, :, zs] = jnp.where(inside, UB[y, :, zs] + c, 0.0)
+
+    halos, blocks = [], []
+    prolong(0)
+    for k in range(nk + 1):
+        if k + 1 < nk:
+            prolong(k + 1)
+        if k < nk:
+            scaled = [residual(F, UC, RHO, CX, cy, sz_ref, y, k) * RD[y, :, cols[k]] for y in range(ny)]
+            solved = smooth_z(scaled, LZ0[k], ny, n)
+            for y in range(ny):
+                UD[y + 1, own, cols[k]] = UC[y + 1, own, cols[k]] + solved[y]
+            halos.append(halo(UD, ny, n, cols[k]))
+        if k > 0:
+            scaled_residual(UD, halos, W2, blocks, k - 1)
+    lx0 = split(LX0[...])
+    stores = []
     for k in range(nk):
-        zs = slice(k * B, k * B + B)
-        scaled = [residual(F, UC, RHO, CX, cy, sz_ref, y, k) * RD[y, :, zs] for y in range(ny)]
-        solved = smooth_z(scaled, lz0_ref[k], ny, n)
-        for y in range(ny):
-            UD[y + 1, own, zs] = UC[y + 1, own, zs] + solved[y]
-        halos.append(halo(UD, ny, n, zs))
-    blocks = exchange_fine(UD, halos, W2)
-    lx0 = split(LX0[...])
-    for k in range(nk):
-        zs = slice(k * B, k * B + B)
         arrive(blocks[k])
         for y in range(ny):
-            OUT[y, :, zs] = UD[y + 1, own, zs] + mm3(lx0, split(W2[y, :, zs]))
-    stores = [pltpu.make_async_copy(OUT.at[y], out_ref.at[:, y, :], ls.at[y]) for y in range(ny)]
-    for store in stores:
-        store.start()
+            OUT[y, :, cols[k]] = UD[y + 1, own, cols[k]] + mm3(lx0, split(W2[y, :, cols[k]]))
+            store = pltpu.make_async_copy(OUT.at[y, :, cols[k]], out_ref.at[:, y, cols[k]], ls.at[len(stores)])
+            store.start()
+            stores.append(store)
     for sends, copy in pending:
         if sends is None:
             copy.wait_send()
@@ -378,27 +453,28 @@
     padded = pltpu.VMEM((ny + 2, n + 2 * H, nz), f32)
     coarse = pltpu.VMEM((ny1, n1, nz1), f32)
     coarse_padded = pltpu.VMEM((ny1 + 2, n1 + 2 * H, nz1), f32)
-    copies = 4 + 12 * nk + 2 * nk * (g - 1) + 4 + 4 * 4 + 4 + 2 * (g1 - 1) + npx + npy - 2
+    copies = 4 + nk * (14 + 2 * g) + nk // 2 * (18 + 2 * g1) + npx + npy - 2
     anywhere = pl.BlockSpec(memory_space=pl.ANY)
     vmem = pl.BlockSpec(memory_space=pltpu.VMEM)
     smem = pl.BlockSpec(memory_space=pltpu.SMEM)
     return pl.pallas_call(
         functools.partial(kernel, (n, ny, nz, B, npx, npy)),
         out_shape=jax.ShapeDtypeStruct(f.shape, f32),
-        in_specs=[anywhere, anywhere, vmem, smem, vmem, vmem, anywhere, vmem, anywhere, vmem],
+        in_specs=[anywhere, anywhere, vmem, smem, vmem, anywhere, anywhere, anywhere, anywhere, vmem],
         out_specs=anywhere,
         scratch_shapes=[
             fine, fine, fine, padded, padded, padded, padded,
             pltpu.VMEM((ny, B, nz), f32), pltpu.VMEM((ny, B, nz), f32),
-            pltpu.VMEM((ny, n + 2 * H, nz), f32), pltpu.VMEM((ny + 2, n1, nz1), f32),
+            pltpu.VMEM((ny, n + 2 * H, nz), f32), pltpu.VMEM((ny, n1, nz), f32), pltpu.VMEM((ny + 2, n1, nz1), f32),
             coarse, coarse, coarse,
             coarse_padded, coarse_padded, coarse_padded, coarse_padded, coarse_padded,
             pltpu.VMEM((ny1, B, nz1), f32), pltpu.VMEM((ny1, B, nz1), f32),
             pltpu.VMEM((npx, 8, lanes), f32), pltpu.VMEM((npy, 8, lanes), f32), pltpu.VMEM((5, 8, lanes), f32),
             pltpu.VMEM((n, B), f32), pltpu.VMEM((n1, B), f32), pltpu.VMEM((8, nz1), f32),
+            pltpu.VMEM(lz0.shape, f32), pltpu.VMEM(lz1.shape, f32),
             pltpu.VMEM((n, B), f32), pltpu.VMEM((n1, B), f32), fine,
             pltpu.SemaphoreType.DMA((copies,)), pltpu.SemaphoreType.DMA((copies,)),
-            pltpu.SemaphoreType.DMA((2 * ny + 2,)),
+            pltpu.SemaphoreType.DMA((nk * (2 * ny + 1) + 3,)),
         ],
         compiler_params=pltpu.CompilerParams(
             collective_id=0, has_side_effects=True, vmem_limit_bytes=56 * 1024 * 1024

time: 122 us -> 125 us (1.025)
  Pallas kernels: 119 us -> 122 us
    pallas_call x1, Pallas kernels: 119 us -> 122 us  [per_device(): pl.pallas_call(functools.partial(kernel, (n, ny, nz, B, npx, npy)), out_s...]
where the time goes in v2:
time: 125 us; the launch traced here: 124 us
  Pallas kernels  122 us (98%)
  local copies, waits for them, and re-layouts  2.26 us (2%)
    pallas_call x1, Pallas kernels, per_device(): pl.pallas_call(functools.partial(kernel, (n, ny, nz, B, npx, npy)), out_s...  122 us

profile of v2, /device:TPU:0, one launch (start us, length us, event | category | flops | bytes accessed | tf_op | source)
XLA Modules:
  0.0 124.4 jit_solution(8362570676999927224)
XLA Ops:
  0.0 122.1 %shard_map.100 = f32[128,2,1024]{2,1,0:T(2,128)} custom-call(f32[128,2,1024]{2,1,0:T(2,128)} %f_in.1, f32[128,2,1024]{2,1,0:T(2,128)} %rho_in.1, f32[1,128]{1,0:T(1,128)} %bitcast.3, f32[2]{0:T(128)} %sy_ref.1, f32[1,1024]{1,0:T(1,128)} %bitcast.2, f32[4,256,256]{2,1,0:T(8,128)} %lz0_in.1, f32[4,256,256]{2,1,0:T(8,128)} %lx0_in.1, f32[2,256,256]{2,1,0:T(8,128)} %lz1_in.1, ...), custom_call_target="tpu_custom_call" | custom-call | tf_op jit(solution)/shard_map/pallas_call | solution.py:460
  122.1 2.3 %copy.12 = f32[128,2,1024]{2,1,0:T(2,128)} copy(f32[128,2,1024]{2,1,0:T(2,128)} %shard_map.100) | data formatting | bytes 2097152

commit v3 on v2

--- a/solution.py
+++ b/solution.py
@@ -26,7 +26,20 @@
 
 def mm3(a, b, transposed=False):
     (ah, al), (bh, bl) = a, b
-    return mm(ah, bh, transposed) + (mm(ah, bl, transposed) + mm(al, bh, transposed))
+    axis = 1 if transposed else 0
+    return mm(
+        jnp.concatenate([ah, ah, al], axis=1), jnp.concatenate([bh, bl, bh], axis=axis), transposed
+    )
+
+
+def strips(rows, body):
+    step = min(rows, 32)
+
+    def at(t, carry):
+        body(pl.multiple_of(t * step, step), step)
+        return carry
+
+    lax.fori_loop(0, rows // step, at, 0)
 
 
 def weights(shape, fine_dim, fine_pad, coarse_pad, inner, outer):
@@ -45,8 +58,9 @@
 
 
 def right_mul(v, m):
-    hi, lo = split(v)
-    return mm(hi, m) + mm(lo, m)
+    rows = v.shape[0]
+    both = mm(jnp.concatenate(split(v), axis=0), m)
+    return both[:rows] + both[rows:]
 
 
 def kernel(
@@ -54,7 +68,7 @@
     f_in, rho_in, sx_ref, sy_ref, sz_ref, lz0_in, lx0_in, lz1_in, lx1_in, c_ref,
     out_ref,
     F, RHO, RD, UA, UB, UC, UD, W, W2, R0, TX, T1, F1, RHO1, RD1,
-    M1, M2, MP, M3, M4, V, V2, G1, G2, CB, CX, CX1, CZ1, LZ0, LZ1, LX0, LX1, OUT,
+    M1, M2, MP, M3, M4, V, V2, G1, G2, CB, CX, CX1, CZ1, LZ0, LZ1, LX0, LX1, SH, SL, OUT,
     ss, rs, ls,
 ):
     n, ny, nz, B, npx, npy = dims
@@ -182,26 +196,30 @@
         mine = ref.at[:, pl.ds(at, rows), zs]
         return [push(mine, mine, base + lax.rem(here + s, peers), j) for s in range(1, peers)]
 
-    def residual(rhs, ref, rho, cx, cys, cz, y, k):
-        rows = rhs.shape[1]
+    def residual(rhs, ref, rho, cx, cys, cz, y, k, r, step):
         lo = k * B
         zs = slice(lo, lo + B)
-        own = slice(H, H + rows)
-        c = ref[y + 1, own, zs]
-        near_x = ref[y + 1, H - 1:H - 1 + rows, zs] + ref[y + 1, H + 1:H + 1 + rows, zs]
+        here = pl.ds(r, step)
+        own = pl.ds(pl.multiple_of(r + H, H), step)
+        block = ref[y + 1, pl.ds(r, step + 2 * H), zs]
+        c = block[H:H + step]
+        near_x = block[H - 1:H - 1 + step] + block[H + 1:H + 1 + step]
         near_y = ref[y, own, zs] + ref[y + 2, own, zs]
-        blank = jnp.zeros((rows, 128), f32)
+        blank = jnp.zeros((step, 128), f32)
         left = ref[y + 1, own, lo - 128:lo] if lo > 0 else blank
         right = ref[y + 1, own, lo + B:lo + B + 128] if lo + B < ref.shape[2] else blank
         wide = jnp.concatenate([left, c, right], axis=1)
         near_z = (pltpu.roll(wide, 1, 1) + pltpu.roll(wide, B + 255, 1))[:, 128:128 + B]
         twice = 2.0 * c
-        stencil = cx[...] * (twice - near_x) + cys[y] * (twice - near_y) + cz[0:1, zs] * (twice - near_z)
-        return rhs[y, :, zs] - (shift_term * c + rho[y, :, zs] * stencil)
-
-    def inverse_diagonal(rho, cx, cys, cz, y, k):
+        stencil = (
+            cx[here, :] * (twice - near_x) + cys[y] * (twice - near_y) + cz[0:1, zs] * (twice - near_z)
+        )
+        return rhs[y, here, zs] - (shift_term * c + rho[y, here, zs] * stencil)
+
+    def inverse_diagonal(rho, cx, cys, cz, y, k, r, step):
         zs = slice(k * B, k * B + B)
-        return 1.0 / (shift_term + 2.0 * rho[y, :, zs] * (cx[...] + cys[y] + cz[0:1, zs]))
+        here = pl.ds(r, step)
+        return 1.0 / (shift_term + 2.0 * rho[y, here, zs] * (cx[here, :] + cys[y] + cz[0:1, zs]))
 
     square = (n, n)
     diag = lax.broadcasted_iota(jnp.int32, square, 0) == lax.broadcasted_iota(jnp.int32, square, 1)
@@ -221,9 +239,12 @@
             push(CB.at[0], CB.at[4], i, ym, has_ym, has_yp),
         ])
 
-    def smooth_z(values, block, planes, rows):
-        w = jnp.concatenate(values, axis=0)
-        z = mm3(split(w), split(block), True)
+    def keep(value, y, rows, r, step):
+        at = pl.ds(pl.multiple_of(y * rows + r, step), step)
+        SH[at, :], SL[at, :] = split(value)
+
+    def smooth_z(block, planes, rows):
+        z = mm3((SH[0:planes * rows], SL[0:planes * rows]), split(block), True)
         return [z[y * rows:(y + 1) * rows] for y in range(planes)]
 
     def window(ref, y, k, width, side):
@@ -241,9 +262,13 @@
 
     def scaled_residual(ref, halos, target, blocks, k):
         arrive(halos[k])
-        for y in range(ny):
-            r = residual(F, ref, RHO, CX, cy, sz_ref, y, k)
-            target[y, pl.ds(at0, n), cols[k]] = r * RD[y, :, cols[k]]
+
+        def body(r, step):
+            for y in range(ny):
+                v = residual(F, ref, RHO, CX, cy, sz_ref, y, k, r, step)
+                target[y, pl.ds(pl.multiple_of(at0 + r, step), step), cols[k]] = v * RD[y, pl.ds(r, step), cols[k]]
+
+        strips(n, body)
         blocks.append(to_block(target, at0, n, g, cols[k]))
 
     halos, blocks = [], []
@@ -251,12 +276,16 @@
         if k < nk:
             for copy in parts[k]:
                 copy.wait()
-            scaled = []
-            for y in range(ny):
-                rd = inverse_diagonal(RHO, CX, cy, sz_ref, y, k)
-                RD[y, :, cols[k]] = rd
-                scaled.append(F[y, :, cols[k]] * rd)
-            solved = smooth_z(scaled, LZ0[k], ny, n)
+
+            def body(r, step, k=k):
+                here = pl.ds(r, step)
+                for y in range(ny):
+                    rd = inverse_diagonal(RHO, CX, cy, sz_ref, y, k, r, step)
+                    RD[y, here, cols[k]] = rd
+                    keep(F[y, here, cols[k]] * rd, y, n, r, step)
+
+            strips(n, body)
+            solved = smooth_z(LZ0[k], ny, n)
             for y in range(ny):
                 UA[y + 1, own, cols[k]] = solved[y]
             if k == 0:
@@ -278,15 +307,24 @@
             RHO1[y, :, k * half:k * half + half] = right_mul(left_mul(mean_x, pair), mean_z)
     for y in range(ny1):
         for k in range(nk1):
-            RD1[y, :, cols[k]] = inverse_diagonal(RHO1, CX1, cy1, CZ1, y, k)
+
+            def body(r, step, y=y, k=k):
+                RD1[y, pl.ds(r, step), cols[k]] = inverse_diagonal(RHO1, CX1, cy1, CZ1, y, k, r, step)
+
+            strips(n1, body)
 
     lx0 = split(LX0[...])
     halos, rims, sides, halos1 = [], [], [], []
 
     def fine_residual(k):
         arrive(halos[k])
-        for y in range(ny):
-            R0[y, own, cols[k]] = residual(F, UB, RHO, CX, cy, sz_ref, y, k)
+
+        def body(r, step):
+            for y in range(ny):
+                v = residual(F, UB, RHO, CX, cy, sz_ref, y, k, r, step)
+                R0[y, pl.ds(pl.multiple_of(r + H, H), step), cols[k]] = v
+
+        strips(n, body)
         rims.append(halo_x(R0, (0, ny), n, cols[k]))
 
     def restrict_rows(k):
@@ -309,8 +347,13 @@
             F1[y, :, cols[k]] = (T1[a, :, cols[k]] + 3.0 * inner + T1[a + 3, :, cols[k]]) * 0.125
 
     def middle_z(ref, before, rhs, k):
-        scaled = [r * RD1[y, :, cols[k]] for y, r in enumerate(rhs)]
-        solved = smooth_z(scaled, LZ1[k], ny1, n1)
+
+        def body(r, step):
+            for y in range(ny1):
+                keep(rhs(y, r, step) * RD1[y, pl.ds(r, step), cols[k]], y, n1, r, step)
+
+        strips(n1, body)
+        solved = smooth_z(LZ1[k], ny1, n1)
         for y in range(ny1):
             u = solved[y] if before is None else before[y + 1, own1, cols[k]] + solved[y]
             ref[y + 1, own1, cols[k]] = u
@@ -318,7 +361,7 @@
 
     def middle_first(k):
         middle_rhs(k)
-        halos1.append(middle_z(M1, None, [F1[y, :, cols[k]] for y in range(ny1)], k))
+        halos1.append(middle_z(M1, None, lambda y, r, step: F1[y, pl.ds(r, step), cols[k]], k))
 
     for k in range(nk):
         arrive(blocks[k])
@@ -344,9 +387,14 @@
         sent = []
         for k in range(nk1):
             arrive(halos1[k])
-            for y in range(ny1):
-                r = residual(F1, ref, RHO1, CX1, cy1, CZ1, y, k)
-                target[y, pl.ds(at1, n1), cols[k]] = r * RD1[y, :, cols[k]]
+
+            def body(r, step, k=k):
+                for y in range(ny1):
+                    v = residual(F1, ref, RHO1, CX1, cy1, CZ1, y, k, r, step)
+                    at = pl.ds(pl.multiple_of(at1 + r, step), step)
+                    target[y, at, cols[k]] = v * RD1[y, pl.ds(r, step), cols[k]]
+
+            strips(n1, body)
             sent.append(to_block(target, at1, n1, g1, cols[k]))
         edges = []
         for k in range(nk1):
@@ -365,9 +413,16 @@
     total = jnp.zeros((1, B), f32)
     for k in range(nk1):
         arrive(edges[k])
-        for y in range(ny1):
-            r = residual(F1, M2, RHO1, CX1, cy1, CZ1, y, k)
-            total = total + jnp.sum(r, axis=0, keepdims=True)
+        step1 = min(n1, 32)
+
+        def add(t, total, k=k, step1=step1):
+            r = pl.multiple_of(t * step1, step1)
+            for y in range(ny1):
+                v = residual(F1, M2, RHO1, CX1, cy1, CZ1, y, k, r, step1)
+                total = total + jnp.sum(v, axis=0, keepdims=True)
+            return total
+
+        total = lax.fori_loop(0, n1 // step1, add, total)
     mean = jnp.sum(total, axis=1, keepdims=True) * (1.0 / (ny1 * n1 * nz1))
     lane = lax.broadcasted_iota(jnp.int32, CB.shape[1:], 1)
     G1[i] = jnp.where(lane == j * npx + i, mean, 0.0)
@@ -385,7 +440,10 @@
 
     halos1 = []
     for k in range(nk1):
-        rhs = [residual(F1, MP, RHO1, CX1, cy1, CZ1, y, k) for y in range(ny1)]
+
+        def rhs(y, r, step, k=k):
+            return residual(F1, MP, RHO1, CX1, cy1, CZ1, y, k, r, step)
+
         halos1.append(middle_z(M3, MP, rhs, k))
     edges = middle_x(M3, halos1, V2, M4, True)
 
@@ -400,7 +458,9 @@
             arrive(edges[len(arrived)])
             arrived.append(k)
         zs = cols[k]
-        raised = [left_mul(raise_x, right_mul(window(M4, y, k, half, 128), raise_z)) for y in range(ny1 + 2)]
+        rows = n1 + 2 * H
+        wide = right_mul(jnp.concatenate([window(M4, y, k, half, 128) for y in range(ny1 + 2)], axis=0), raise_z)
+        raised = [left_mul(raise_x, wide[y * rows:(y + 1) * rows]) for y in range(ny1 + 2)]
         for y in range(ny + 2):
             near = (y - 1) // 2 + 1
             other = near - 1 if (y - 1) % 2 == 0 else near + 1
@@ -418,8 +478,14 @@
         if k + 1 < nk:
             prolong(k + 1)
         if k < nk:
-            scaled = [residual(F, UC, RHO, CX, cy, sz_ref, y, k) * RD[y, :, cols[k]] for y in range(ny)]
-            solved = smooth_z(scaled, LZ0[k], ny, n)
+
+            def body(r, step, k=k):
+                for y in range(ny):
+                    v = residual(F, UC, RHO, CX, cy, sz_ref, y, k, r, step)
+                    keep(v * RD[y, pl.ds(r, step), cols[k]], y, n, r, step)
+
+            strips(n, body)
+            solved = smooth_z(LZ0[k], ny, n)
             for y in range(ny):
                 UD[y + 1, own, cols[k]] = UC[y + 1, own, cols[k]] + solved[y]
             halos.append(halo(UD, ny, n, cols[k]))
@@ -472,7 +538,8 @@
             pltpu.VMEM((npx, 8, lanes), f32), pltpu.VMEM((npy, 8, lanes), f32), pltpu.VMEM((5, 8, lanes), f32),
             pltpu.VMEM((n, B), f32), pltpu.VMEM((n1, B), f32), pltpu.VMEM((8, nz1), f32),
             pltpu.VMEM(lz0.shape, f32), pltpu.VMEM(lz1.shape, f32),
-            pltpu.VMEM((n, B), f32), pltpu.VMEM((n1, B), f32), fine,
+            pltpu.VMEM((n, B), f32), pltpu.VMEM((n1, B), f32),
+            pltpu.VMEM((ny * n, B), bf16), pltpu.VMEM((ny * n, B), bf16), fine,
             pltpu.SemaphoreType.DMA((copies,)), pltpu.SemaphoreType.DMA((copies,)),
             pltpu.SemaphoreType.DMA((nk * (2 * ny + 1) + 3,)),
         ],

time: 125 us -> 126 us (level)
  Pallas kernels: 122 us -> 124 us
    pallas_call x1, Pallas kernels: 122 us -> 124 us  [per_device(): pl.pallas_call(functools.partial(kernel, (n, ny, nz, B, npx, npy)), out_s...]
where the time goes in v3:
time: 126 us
  Pallas kernels  124 us (98%)
  local copies, waits for them, and re-layouts  2.26 us (2%)
    pallas_call x1, Pallas kernels, per_device(): pl.pallas_call(functools.partial(kernel, (n, ny, nz, B, npx, npy)), out_s...  124 us

profile of v3, /device:TPU:0, one launch (start us, length us, event | category | flops | bytes accessed | tf_op | source)
XLA Modules:
  0.0 126.1 jit_solution(14233057565310031351)
XLA Ops:
  0.0 123.8 %shard_map.100 = f32[128,2,1024]{2,1,0:T(2,128)} custom-call(f32[128,2,1024]{2,1,0:T(2,128)} %f_in.1, f32[128,2,1024]{2,1,0:T(2,128)} %rho_in.1, f32[1,128]{1,0:T(1,128)} %bitcast.3, f32[2]{0:T(128)} %sy_ref.1, f32[1,1024]{1,0:T(1,128)} %bitcast.2, f32[4,256,256]{2,1,0:T(8,128)} %lz0_in.1, f32[4,256,256]{2,1,0:T(8,128)} %lx0_in.1, f32[2,256,256]{2,1,0:T(8,128)} %lz1_in.1, ...), custom_call_target="tpu_custom_call" | custom-call | tf_op jit(solution)/shard_map/pallas_call | solution.py:526
  123.8 2.3 %copy.12 = f32[128,2,1024]{2,1,0:T(2,128)} copy(f32[128,2,1024]{2,1,0:T(2,128)} %shard_map.100) | data formatting | bytes 2097152

commit v4 on v3

--- a/solution.py
+++ b/solution.py
@@ -157,11 +157,27 @@
         return receives, copy
 
     def arrive(handles):
-        for receives, copy in handles:
+        while handles:
+            receives, copy = handles.pop(0)
             if receives is None:
                 copy.wait_recv()
             else:
                 pl.when(receives)(copy.wait_recv)
+
+    drained = []
+
+    def drain(until):
+        for sends, copy in pending[len(drained):until]:
+            drained.append(copy)
+            if sends is None:
+                copy.wait_send()
+            else:
+                pl.when(sends)(copy.wait_send)
+
+    def grouped(groups, width, k, handles, start):
+        for a, b in groups:
+            if k == b - 1:
+                handles.extend([start(slice(a * width, b * width))] * (b - a))
 
     def halo_x(ref, planes, rows, zs):
         a, b = planes
@@ -271,28 +287,32 @@
         strips(n, body)
         blocks.append(to_block(target, at0, n, g, cols[k]))
 
+    early = max(1, nk - 2)
+    first_alone = [(0, 1), (1, nk)]
+
     halos, blocks = [], []
-    for k in range(nk + 1):
-        if k < nk:
-            for copy in parts[k]:
-                copy.wait()
-
-            def body(r, step, k=k):
-                here = pl.ds(r, step)
-                for y in range(ny):
-                    rd = inverse_diagonal(RHO, CX, cy, sz_ref, y, k, r, step)
-                    RD[y, here, cols[k]] = rd
-                    keep(F[y, here, cols[k]] * rd, y, n, r, step)
-
-            strips(n, body)
-            solved = smooth_z(LZ0[k], ny, n)
+    for k in range(nk):
+        for copy in parts[k]:
+            copy.wait()
+
+        def body(r, step, k=k):
+            here = pl.ds(r, step)
             for y in range(ny):
-                UA[y + 1, own, cols[k]] = solved[y]
-            if k == 0:
-                enter()
-            halos.append(halo(UA, ny, n, cols[k]))
-        if k > 0:
-            scaled_residual(UA, halos, W, blocks, k - 1)
+                rd = inverse_diagonal(RHO, CX, cy, sz_ref, y, k, r, step)
+                RD[y, here, cols[k]] = rd
+                keep(F[y, here, cols[k]] * rd, y, n, r, step)
+
+        strips(n, body)
+        solved = smooth_z(LZ0[k], ny, n)
+        for y in range(ny):
+            UA[y + 1, own, cols[k]] = solved[y]
+        if k == 0:
+            enter()
+        grouped(first_alone, B, k, halos, lambda zs: halo(UA, ny, n, zs))
+        if k == early:
+            scaled_residual(UA, halos, W, blocks, 0)
+    for k in range(1, nk):
+        scaled_residual(UA, halos, W, blocks, k)
 
     for copy in late:
         copy.wait()
@@ -314,7 +334,7 @@
             strips(n1, body)
 
     lx0 = split(LX0[...])
-    halos, rims, sides, halos1 = [], [], [], []
+    halos, rims, sides = [], [], []
 
     def fine_residual(k):
         arrive(halos[k])
@@ -325,7 +345,7 @@
                 R0[y, pl.ds(pl.multiple_of(r + H, H), step), cols[k]] = v
 
         strips(n, body)
-        rims.append(halo_x(R0, (0, ny), n, cols[k]))
+        grouped([(0, nk - 1), (nk - 1, nk)], B, k, rims, lambda zs: halo_x(R0, (0, ny), n, zs))
 
     def restrict_rows(k):
         arrive(rims[k])
@@ -336,7 +356,8 @@
         zs = slice(k * half, k * half + half)
         for y in range(ny):
             T1[y + 1, :, zs] = right_mul(window(TX, y, k, B, 128), restrict_z)
-        sides.append(halo_y(T1, ny, slice(None), zs))
+        groups = [(0, nk - 2), (nk - 2, nk)]
+        grouped(groups, half, k, sides, lambda at: halo_y(T1, ny, slice(None), at))
 
     def middle_rhs(k):
         arrive(sides[2 * k])
@@ -357,36 +378,38 @@
         for y in range(ny1):
             u = solved[y] if before is None else before[y + 1, own1, cols[k]] + solved[y]
             ref[y + 1, own1, cols[k]] = u
-        return halo(ref, ny1, n1, cols[k])
 
     def middle_first(k):
         middle_rhs(k)
-        halos1.append(middle_z(M1, None, lambda y, r, step: F1[y, pl.ds(r, step), cols[k]], k))
+        middle_z(M1, None, lambda y, r, step: F1[y, pl.ds(r, step), cols[k]], k)
 
     for k in range(nk):
         arrive(blocks[k])
         for y in range(ny):
             UB[y + 1, own, cols[k]] = UA[y + 1, own, cols[k]] + mm3(lx0, split(W[y, :, cols[k]]))
-        halos.append(halo(UB, ny, n, cols[k]))
-        if k >= 1:
-            fine_residual(k - 1)
-            restrict_rows(k - 1)
-        if k >= 2:
-            restrict_columns(k - 2)
+        grouped([(0, nk - 2), (nk - 2, nk - 1), (nk - 1, nk)], B, k, halos, lambda zs: halo(UB, ny, n, zs))
+        if k == nk - 2:
+            for m in range(nk - 2):
+                fine_residual(m)
+    fine_residual(nk - 2)
     fine_residual(nk - 1)
-    for k in range(nk1 - 1):
-        middle_first(k)
+    for k in range(nk - 1):
+        restrict_rows(k)
+    for k in range(nk - 2):
+        restrict_columns(k)
     restrict_rows(nk - 1)
     restrict_columns(nk - 2)
     restrict_columns(nk - 1)
-    middle_first(nk1 - 1)
+    for k in range(nk1):
+        middle_first(k)
 
     lx1 = split(LX1[...])
 
-    def middle_x(ref, halos1, target, result, diagonals):
-        sent = []
+    whole = slice(None)
+
+    def middle_x(ref, target, result):
+        arrive(halo(ref, ny1, n1, whole))
         for k in range(nk1):
-            arrive(halos1[k])
 
             def body(r, step, k=k):
                 for y in range(ny1):
@@ -395,24 +418,18 @@
                     target[y, at, cols[k]] = v * RD1[y, pl.ds(r, step), cols[k]]
 
             strips(n1, body)
-            sent.append(to_block(target, at1, n1, g1, cols[k]))
-        edges = []
+        arrive(to_block(target, at1, n1, g1, whole))
         for k in range(nk1):
-            arrive(sent[k])
             for y in range(ny1):
                 solved = mm3(lx1, split(target[y, :, cols[k]]))
                 result[y + 1, own1, cols[k]] = ref[y + 1, own1, cols[k]] + solved
-            edge = halo(result, ny1, n1, cols[k])
-            if diagonals:
-                edge = edge + halo_corners(result, ny1, n1, cols[k])
-            edges.append(edge)
-        return edges
-
-    edges = middle_x(M1, halos1, V, M2, False)
+        return halo(result, ny1, n1, whole)
+
+    edges = middle_x(M1, V, M2)
+    arrive(edges)
 
     total = jnp.zeros((1, B), f32)
     for k in range(nk1):
-        arrive(edges[k])
         step1 = min(n1, 32)
 
         def add(t, total, k=k, step1=step1):
@@ -438,25 +455,21 @@
     MP[0, own1, :] = M2[0, own1, :] + e[3]
     MP[ny1 + 1, own1, :] = M2[ny1 + 1, own1, :] + e[4]
 
-    halos1 = []
     for k in range(nk1):
 
         def rhs(y, r, step, k=k):
             return residual(F1, MP, RHO1, CX1, cy1, CZ1, y, k, r, step)
 
-        halos1.append(middle_z(M3, MP, rhs, k))
-    edges = middle_x(M3, halos1, V2, M4, True)
+        middle_z(M3, MP, rhs, k)
+    edges = middle_x(M3, V2, M4) + halo_corners(M4, ny1, n1, whole)
 
     raise_x = weights((n + 2 * H, n1 + 2 * H), 0, H, H, 0.75, 0.25)
     raise_z = weights((half + 256, B), 1, 0, 128, 0.75, 0.25)
     row = lax.broadcasted_iota(jnp.int32, (n + 2 * H, 1), 0)
     inside = jnp.logical_and(jnp.logical_or(row >= H, has_xm), jnp.logical_or(row < n + H, has_xp))
-    arrived = []
+    arrive(edges)
 
     def prolong(k):
-        while len(arrived) < min(k + 1, nk - 1) // 2 + 1:
-            arrive(edges[len(arrived)])
-            arrived.append(k)
         zs = cols[k]
         rows = n1 + 2 * H
         wide = right_mul(jnp.concatenate([window(M4, y, k, half, 128) for y in range(ny1 + 2)], axis=0), raise_z)
@@ -474,23 +487,26 @@
 
     halos, blocks = [], []
     prolong(0)
-    for k in range(nk + 1):
+    for k in range(nk):
         if k + 1 < nk:
             prolong(k + 1)
-        if k < nk:
-
-            def body(r, step, k=k):
-                for y in range(ny):
-                    v = residual(F, UC, RHO, CX, cy, sz_ref, y, k, r, step)
-                    keep(v * RD[y, pl.ds(r, step), cols[k]], y, n, r, step)
-
-            strips(n, body)
-            solved = smooth_z(LZ0[k], ny, n)
+
+        def body(r, step, k=k):
             for y in range(ny):
-                UD[y + 1, own, cols[k]] = UC[y + 1, own, cols[k]] + solved[y]
-            halos.append(halo(UD, ny, n, cols[k]))
-        if k > 0:
-            scaled_residual(UD, halos, W2, blocks, k - 1)
+                v = residual(F, UC, RHO, CX, cy, sz_ref, y, k, r, step)
+                keep(v * RD[y, pl.ds(r, step), cols[k]], y, n, r, step)
+
+        strips(n, body)
+        solved = smooth_z(LZ0[k], ny, n)
+        for y in range(ny):
+            UD[y + 1, own, cols[k]] = UC[y + 1, own, cols[k]] + solved[y]
+        grouped(first_alone, B, k, halos, lambda zs: halo(UD, ny, n, zs))
+        if k == early:
+            scaled_residual(UD, halos, W2, blocks, 0)
+    before = len(pending)
+    for k in range(1, nk):
+        scaled_residual(UD, halos, W2, blocks, k)
+    drain(before - (g - 1))
     lx0 = split(LX0[...])
     stores = []
     for k in range(nk):
@@ -500,11 +516,7 @@
             store = pltpu.make_async_copy(OUT.at[y, :, cols[k]], out_ref.at[:, y, cols[k]], ls.at[len(stores)])
             store.start()
             stores.append(store)
-    for sends, copy in pending:
-        if sends is None:
-            copy.wait_send()
-        else:
-            pl.when(sends)(copy.wait_send)
+    drain(len(pending))
     for store in stores:
         store.wait()
 

time: 126 us -> 131 us (1.040)
  Pallas kernels: 124 us -> 128 us
    pallas_call x1, Pallas kernels: 124 us -> 128 us  [per_device(): pl.pallas_call(functools.partial(kernel, (n, ny, nz, B, npx, npy)), out_s...]
where the time goes in v4:
time: 131 us
  Pallas kernels  128 us (98%)
  local copies, waits for them, and re-layouts  2.26 us (2%)
    pallas_call x1, Pallas kernels, per_device(): pl.pallas_call(functools.partial(kernel, (n, ny, nz, B, npx, npy)), out_s...  128 us

profile of v4, /device:TPU:0, one launch (start us, length us, event | category | flops | bytes accessed | tf_op | source)
XLA Modules:
  0.0 130.7 jit_solution(9811050909226437162)
XLA Ops:
  0.0 128.5 %shard_map.100 = f32[128,2,1024]{2,1,0:T(2,128)} custom-call(f32[128,2,1024]{2,1,0:T(2,128)} %f_in.1, f32[128,2,1024]{2,1,0:T(2,128)} %rho_in.1, f32[1,128]{1,0:T(1,128)} %bitcast.3, f32[2]{0:T(128)} %sy_ref.1, f32[1,1024]{1,0:T(1,128)} %bitcast.2, f32[4,256,256]{2,1,0:T(8,128)} %lz0_in.1, f32[4,256,256]{2,1,0:T(8,128)} %lx0_in.1, f32[2,256,256]{2,1,0:T(8,128)} %lz1_in.1, ...), custom_call_target="tpu_custom_call" | custom-call | tf_op jit(solution)/shard_map/pallas_call | solution.py:538
  128.5 2.3 %copy.12 = f32[128,2,1024]{2,1,0:T(2,128)} copy(f32[128,2,1024]{2,1,0:T(2,128)} %shard_map.100) | data formatting | bytes 2097152

commit v5 on v2

--- a/solution.py
+++ b/solution.py
@@ -54,7 +54,7 @@
     f_in, rho_in, sx_ref, sy_ref, sz_ref, lz0_in, lx0_in, lz1_in, lx1_in, c_ref,
     out_ref,
     F, RHO, RD, UA, UB, UC, UD, W, W2, R0, TX, T1, F1, RHO1, RD1,
-    M1, M2, MP, M3, M4, V, V2, G1, G2, CB, CX, CX1, CZ1, LZ0, LZ1, LX0, LX1, OUT,
+    M1, M2, MP, M3, M4, V, V2, G1, G2, CB, CX, CX1, CZ1, LZ0, LZ1, LX0, LX1, FS, RS,
     ss, rs, ls,
 ):
     n, ny, nz, B, npx, npy = dims
@@ -77,13 +77,11 @@
 
     half = B // 2
     cols = [slice(k * B, k * B + B) for k in range(nk)]
-    parts = []
-    for k in range(nk):
-        part = [load(lz0_in.at[k], LZ0.at[k])]
-        for y in range(ny):
-            part.append(load(f_in.at[:, y, cols[k]], F.at[y, :, cols[k]]))
-            part.append(load(rho_in.at[:, y, cols[k]], RHO.at[y, :, cols[k]]))
-        parts.append(part)
+    tiles = nz // 128
+    first_loads = [load(rho_in, RS), load(f_in, FS), load(lz0_in, LZ0)]
+
+    def rows_of(y, tile):
+        return pl.ds(tile * ny + y, n, stride=tiles * ny)
     at0 = pl.multiple_of(lax.rem(i, g) * n, n)
     at1 = pl.multiple_of(lax.rem(i, g1) * n1, n1)
     late = [
@@ -148,6 +146,12 @@
                 copy.wait_recv()
             else:
                 pl.when(receives)(copy.wait_recv)
+
+    def sent(sends, copy):
+        if sends is None:
+            copy.wait_send()
+        else:
+            pl.when(sends)(copy.wait_send)
 
     def halo_x(ref, planes, rows, zs):
         a, b = planes
@@ -249,8 +253,13 @@
     halos, blocks = [], []
     for k in range(nk + 1):
         if k < nk:
-            for copy in parts[k]:
-                copy.wait()
+            if k == 0:
+                for copy in first_loads:
+                    copy.wait()
+            for tile in range(k * B // 128, (k + 1) * B // 128):
+                for y in range(ny):
+                    F[y, :, tile * 128:tile * 128 + 128] = FS[rows_of(y, tile), :]
+                    RHO[y, :, tile * 128:tile * 128 + 128] = RS[rows_of(y, tile), :]
             scaled = []
             for y in range(ny):
                 rd = inverse_diagonal(RHO, CX, cy, sz_ref, y, k)
@@ -412,6 +421,7 @@
             else:
                 UC[y, :, zs] = jnp.where(inside, UB[y, :, zs] + c, 0.0)
 
+    settled = len(pending)
     halos, blocks = [], []
     prolong(0)
     for k in range(nk + 1):
@@ -426,21 +436,19 @@
         if k > 0:
             scaled_residual(UD, halos, W2, blocks, k - 1)
     lx0 = split(LX0[...])
-    stores = []
+    for sends, copy in pending[:settled]:
+        sent(sends, copy)
     for k in range(nk):
         arrive(blocks[k])
         for y in range(ny):
-            OUT[y, :, cols[k]] = UD[y + 1, own, cols[k]] + mm3(lx0, split(W2[y, :, cols[k]]))
-            store = pltpu.make_async_copy(OUT.at[y, :, cols[k]], out_ref.at[:, y, cols[k]], ls.at[len(stores)])
-            store.start()
-            stores.append(store)
-    for sends, copy in pending:
-        if sends is None:
-            copy.wait_send()
-        else:
-            pl.when(sends)(copy.wait_send)
-    for store in stores:
-        store.wait()
+            result = UD[y + 1, own, cols[k]] + mm3(lx0, split(W2[y, :, cols[k]]))
+            for t in range(B // 128):
+                FS[rows_of(y, k * B // 128 + t), :] = result[:, t * 128:t * 128 + 128]
+    store = pltpu.make_async_copy(FS, out_ref, ls.at[0])
+    store.start()
+    for sends, copy in pending[settled:]:
+        sent(sends, copy)
+    store.wait()
 
 
 def per_device(npx, npy, f, rho, sx, sy, sz, lz0, lx0, lz1, lx1, c):
@@ -449,17 +457,22 @@
     n1, ny1, nz1 = n // 2, ny // 2, nz // 2
     g, g1, nk = B // n, B // n1, nz // B
     lanes = -(-c.shape[1] // 128) * 128
+    linear = pltpu.VMEM((n * nz // 128 * ny, 128), f32)
     fine = pltpu.VMEM((ny, n, nz), f32)
     padded = pltpu.VMEM((ny + 2, n + 2 * H, nz), f32)
     coarse = pltpu.VMEM((ny1, n1, nz1), f32)
     coarse_padded = pltpu.VMEM((ny1 + 2, n1 + 2 * H, nz1), f32)
     copies = 4 + nk * (14 + 2 * g) + nk // 2 * (18 + 2 * g1) + npx + npy - 2
+
+    def rows(field):
+        return field.reshape(n, ny, nz // 128, 128).transpose(0, 2, 1, 3).reshape(-1, 128)
+
     anywhere = pl.BlockSpec(memory_space=pl.ANY)
     vmem = pl.BlockSpec(memory_space=pltpu.VMEM)
     smem = pl.BlockSpec(memory_space=pltpu.SMEM)
-    return pl.pallas_call(
+    out = pl.pallas_call(
         functools.partial(kernel, (n, ny, nz, B, npx, npy)),
-        out_shape=jax.ShapeDtypeStruct(f.shape, f32),
+        out_shape=jax.ShapeDtypeStruct((n * nz // 128 * ny, 128), f32),
         in_specs=[anywhere, anywhere, vmem, smem, vmem, anywhere, anywhere, anywhere, anywhere, vmem],
         out_specs=anywhere,
         scratch_shapes=[
@@ -472,14 +485,15 @@
             pltpu.VMEM((npx, 8, lanes), f32), pltpu.VMEM((npy, 8, lanes), f32), pltpu.VMEM((5, 8, lanes), f32),
             pltpu.VMEM((n, B), f32), pltpu.VMEM((n1, B), f32), pltpu.VMEM((8, nz1), f32),
             pltpu.VMEM(lz0.shape, f32), pltpu.VMEM(lz1.shape, f32),
-            pltpu.VMEM((n, B), f32), pltpu.VMEM((n1, B), f32), fine,
+            pltpu.VMEM((n, B), f32), pltpu.VMEM((n1, B), f32), linear, linear,
             pltpu.SemaphoreType.DMA((copies,)), pltpu.SemaphoreType.DMA((copies,)),
-            pltpu.SemaphoreType.DMA((nk * (2 * ny + 1) + 3,)),
+            pltpu.SemaphoreType.DMA((6,)),
         ],
         compiler_params=pltpu.CompilerParams(
             collective_id=0, has_side_effects=True, vmem_limit_bytes=56 * 1024 * 1024
         ),
-    )(f, rho, sx.reshape(1, n), sy, sz.reshape(1, nz), lz0, lx0, lz1, lx1, c)
+    )(rows(f), rows(rho), sx.reshape(1, n), sy, sz.reshape(1, nz), lz0, lx0, lz1, lx1, c)
+    return out.reshape(n, nz // 128, ny, 128).transpose(0, 2, 1, 3).reshape(n, ny, nz)
 
 
 def solution(mesh):

time: 125 us -> 125 us (level)
  no operation moved by 1% of the time
where the time goes in v5:
time: 125 us; the launch traced here: 124 us
  Pallas kernels  122 us (98%)
  local copies, waits for them, and re-layouts  2.26 us (2%)
    pallas_call x1, Pallas kernels, per_device(): pl.pallas_call(functools.partial(kernel, (n, ny, nz, B, npx, npy)), out_s...  122 us

profile of v5, /device:TPU:0, one launch (start us, length us, event | category | flops | bytes accessed | tf_op | source)
XLA Modules:
  0.0 124.3 jit_solution(11573405750442945556)
XLA Ops:
  0.0 122.0 %shard_map.100 = f32[2048,128]{1,0:T(8,128)} custom-call(f32[2048,128]{1,0:T(8,128)} %bitcast.18, f32[2048,128]{1,0:T(8,128)} %bitcast.19, f32[1,128]{1,0:T(1,128)} %bitcast.21, f32[2]{0:T(128)} %sy_ref.1, f32[1,1024]{1,0:T(1,128)} %bitcast.20, f32[4,256,256]{2,1,0:T(8,128)} %lz0_in.1, f32[4,256,256]{2,1,0:T(8,128)} %lx0_in.1, f32[2,256,256]{2,1,0:T(8,128)} %lz1_in.1, ...), custom_call_target="tpu_custom_call" | custom-call | tf_op jit(solution)/shard_map/pallas_call | solution.py:473
  122.0 2.3 %copy.15 = f32[128,2,1024]{2,1,0:T(2,128)} copy(f32[128,2,1024]{2,1,0:T(2,128)} %bitcast.17) | data formatting | bytes 2097152

commit v6 on v5

--- a/solution.py
+++ b/solution.py
@@ -251,28 +251,27 @@
         blocks.append(to_block(target, at0, n, g, cols[k]))
 
     halos, blocks = [], []
-    for k in range(nk + 1):
-        if k < nk:
-            if k == 0:
-                for copy in first_loads:
-                    copy.wait()
-            for tile in range(k * B // 128, (k + 1) * B // 128):
-                for y in range(ny):
-                    F[y, :, tile * 128:tile * 128 + 128] = FS[rows_of(y, tile), :]
-                    RHO[y, :, tile * 128:tile * 128 + 128] = RS[rows_of(y, tile), :]
-            scaled = []
+    for k in range(nk):
+        if k == 0:
+            for copy in first_loads:
+                copy.wait()
+        for tile in range(k * B // 128, (k + 1) * B // 128):
             for y in range(ny):
-                rd = inverse_diagonal(RHO, CX, cy, sz_ref, y, k)
-                RD[y, :, cols[k]] = rd
-                scaled.append(F[y, :, cols[k]] * rd)
-            solved = smooth_z(scaled, LZ0[k], ny, n)
-            for y in range(ny):
-                UA[y + 1, own, cols[k]] = solved[y]
-            if k == 0:
-                enter()
-            halos.append(halo(UA, ny, n, cols[k]))
-        if k > 0:
-            scaled_residual(UA, halos, W, blocks, k - 1)
+                F[y, :, tile * 128:tile * 128 + 128] = FS[rows_of(y, tile), :]
+                RHO[y, :, tile * 128:tile * 128 + 128] = RS[rows_of(y, tile), :]
+        scaled = []
+        for y in range(ny):
+            rd = inverse_diagonal(RHO, CX, cy, sz_ref, y, k)
+            RD[y, :, cols[k]] = rd
+            scaled.append(F[y, :, cols[k]] * rd)
+        solved = smooth_z(scaled, LZ0[k], ny, n)
+        for y in range(ny):
+            UA[y + 1, own, cols[k]] = solved[y]
+        if k == 0:
+            enter()
+        halos.append(halo(UA, ny, n, cols[k]))
+    for k in range(nk):
+        scaled_residual(UA, halos, W, blocks, k)
 
     for copy in late:
         copy.wait()
@@ -334,18 +333,14 @@
         for y in range(ny):
             UB[y + 1, own, cols[k]] = UA[y + 1, own, cols[k]] + mm3(lx0, split(W[y, :, cols[k]]))
         halos.append(halo(UB, ny, n, cols[k]))
-        if k >= 1:
-            fine_residual(k - 1)
-            restrict_rows(k - 1)
-        if k >= 2:
-            restrict_columns(k - 2)
-    fine_residual(nk - 1)
-    for k in range(nk1 - 1):
+    for k in range(nk):
+        fine_residual(k)
+    for k in range(nk):
+        restrict_rows(k)
+    for k in range(nk):
+        restrict_columns(k)
+    for k in range(nk1):
         middle_first(k)
-    restrict_rows(nk - 1)
-    restrict_columns(nk - 2)
-    restrict_columns(nk - 1)
-    middle_first(nk1 - 1)
 
     lx1 = split(LX1[...])
 
@@ -424,17 +419,16 @@
     settled = len(pending)
     halos, blocks = [], []
     prolong(0)
-    for k in range(nk + 1):
+    for k in range(nk):
         if k + 1 < nk:
             prolong(k + 1)
-        if k < nk:
-            scaled = [residual(F, UC, RHO, CX, cy, sz_ref, y, k) * RD[y, :, cols[k]] for y in range(ny)]
-            solved = smooth_z(scaled, LZ0[k], ny, n)
-            for y in range(ny):
-                UD[y + 1, own, cols[k]] = UC[y + 1, own, cols[k]] + solved[y]
-            halos.append(halo(UD, ny, n, cols[k]))
-        if k > 0:
-            scaled_residual(UD, halos, W2, blocks, k - 1)
+        scaled = [residual(F, UC, RHO, CX, cy, sz_ref, y, k) * RD[y, :, cols[k]] for y in range(ny)]
+        solved = smooth_z(scaled, LZ0[k], ny, n)
+        for y in range(ny):
+            UD[y + 1, own, cols[k]] = UC[y + 1, own, cols[k]] + solved[y]
+        halos.append(halo(UD, ny, n, cols[k]))
+    for k in range(nk):
+        scaled_residual(UD, halos, W2, blocks, k)
     lx0 = split(LX0[...])
     for sends, copy in pending[:settled]:
         sent(sends, copy)

time: 125 us -> 118 us (0.944)
  Pallas kernels: 122 us -> 116 us
    pallas_call x1, Pallas kernels: 122 us -> 116 us  [per_device(): pl.pallas_call(functools.partial(kernel, (n, ny, nz, B, npx, npy)), out_s...]
where the time goes in v6:
time: 118 us
  Pallas kernels  116 us (98%)
  local copies, waits for them, and re-layouts  2.26 us (2%)
    pallas_call x1, Pallas kernels, per_device(): pl.pallas_call(functools.partial(kernel, (n, ny, nz, B, npx, npy)), out_s...  116 us

profile of v6, /device:TPU:0, one launch (start us, length us, event | category | flops | bytes accessed | tf_op | source)
XLA Modules:
  0.0 117.9 jit_solution(814757630515308117)
XLA Ops:
  0.0 115.7 %shard_map.100 = f32[2048,128]{1,0:T(8,128)} custom-call(f32[2048,128]{1,0:T(8,128)} %bitcast.18, f32[2048,128]{1,0:T(8,128)} %bitcast.19, f32[1,128]{1,0:T(1,128)} %bitcast.21, f32[2]{0:T(128)} %sy_ref.1, f32[1,1024]{1,0:T(1,128)} %bitcast.20, f32[4,256,256]{2,1,0:T(8,128)} %lz0_in.1, f32[4,256,256]{2,1,0:T(8,128)} %lx0_in.1, f32[2,256,256]{2,1,0:T(8,128)} %lz1_in.1, ...), custom_call_target="tpu_custom_call" | custom-call | tf_op jit(solution)/shard_map/pallas_call | solution.py:467
  115.7 2.3 %copy.15 = f32[128,2,1024]{2,1,0:T(2,128)} copy(f32[128,2,1024]{2,1,0:T(2,128)} %bitcast.17) | data formatting | bytes 2097152
